TPU v7x, 32 devices: a whole 2x2x4 slice. The times are simulated.
32 devices in a mesh: row: 8 (over y, x, core), col: 4 (over z).
Axes of the slice: x: 2, y: 2, z: 4, core: 2. Of those that a mesh axis runs over, the one named last changes fastest.
Arguments:
- gain_pair: float32 [2], replicated, may hold values from 0.5 to 2
- weight_up: bfloat16 [24576, 6144], P('row', 'col'), as said below
- weight_down: bfloat16 [6144, 24576], P('row', 'col'), as said below
- inputs_up: bfloat16 [1536, 6144], P('row', 'col'), may hold values from -8 to 8, as said below
- grads_up: bfloat16 [1536, 24576], P('col', 'row'), may hold values from -0.125 to 0.125, as said below
- inputs_down: bfloat16 [1536, 24576], P('row', 'col'), may hold values from -8 to 8, as said below
- grads_down: bfloat16 [1536, 6144], P('col', 'row'), may hold values from -0.125 to 0.125, as said below
- vector_up: float32 [6144], P('col'), may hold values from -6 to 6
- vector_down: float32 [24576], P('col'), may hold values from -6 to 6
Outputs:
- wgrad_up: bfloat16 [24576, 6144], P('row', 'col')
- wgrad_down: bfloat16 [6144, 24576], P('row', 'col')
- gain_grads: float32 [2], replicated
- left_up: float32 [24576], P('row')
- right_up: float32 [6144], P('col')
- left_down: float32 [6144], P('row')
- right_down: float32 [24576], P('col')
Inputs may be any that keep to these rules, and one draw needn't show every extreme that they name: `weight_up`: drawn afresh from the seed for every entry. `weight_down`: drawn afresh from the seed for every entry. `inputs_up`: drawn afresh from the seed for every entry. `inputs_down`: drawn afresh from the seed for every entry. `grads_up`: drawn afresh from the seed for every entry. `grads_down`: drawn afresh from the seed for every entry.
All inputs are finite; a program needn't handle non-finite values.
Results may differ from a plain program's by a relative error of at most 0.007.
Values may be sent and summed in bfloat16 or wider, within the bound.
No kernel may reach another device: no remote copies, remote signals or barrier semaphores. Data moves between devices by JAX's collectives and lax.ppermute only.
A program may use at most 192 MiB of HBM per device.

v0:
```python
import jax
import jax.numpy as jnp
from jax import lax
from jax.sharding import PartitionSpec as P

ITERS = 2


def contract(first, second):
    return lax.dot_general(
        first, second, (((0,), (0,)), ((), ())), preferred_element_type=jnp.float32
    )


def local(
    gain_pair,
    weight_up,
    weight_down,
    inputs_up,
    grads_up,
    inputs_down,
    grads_down,
    vector_up,
    vector_down,
):
    weights = (weight_up, weight_down)
    inputs_all = (
        lax.all_gather(inputs_up, "row", axis=0, tiled=True),
        lax.all_gather(inputs_down, "row", axis=0, tiled=True),
    )
    slice_up = inputs_all[0]
    slice_down = inputs_all[1]
    wsum_up = contract(lax.all_gather(grads_up, "col", axis=0, tiled=True), slice_up)
    wsum_down = contract(lax.all_gather(grads_down, "col", axis=0, tiled=True), slice_down)
    grad_ws = (wsum_up, wsum_down)
    local_inner = tuple((jnp.sum(grad_ws[k] * weights[k].astype(jnp.float32)) for k in range(2)))
    right = (vector_up, vector_down)
    lefts = right
    left_b = right
    sigma = (jnp.float32(1.0), jnp.float32(1.0))
    inner = local_inner
    for step in range(ITERS):
        right_b = tuple((right[k].astype(jnp.bfloat16) for k in range(2)))
        partial_s = tuple(
            (jnp.dot(weights[k], right_b[k], preferred_element_type=jnp.float32) for k in range(2))
        )
        prod_s = lax.psum(partial_s, "col")
        squares = lax.psum((jnp.sum(prod_s[0] * prod_s[0]), jnp.sum(prod_s[1] * prod_s[1])), "row")
        lefts = tuple((prod_s[k] / jnp.sqrt(squares[k] + 1e-06) for k in range(2)))
        left_b = tuple((lefts[k].astype(jnp.bfloat16) for k in range(2)))
        partial_t = tuple(
            (jnp.dot(left_b[k], weights[k], preferred_element_type=jnp.float32) for k in range(2))
        )
        prod_t = lax.psum(partial_t, "row")
        if step + 1 < ITERS:
            right = prod_t
        else:
            local_sq = (jnp.sum(prod_t[0] * prod_t[0]), jnp.sum(prod_t[1] * prod_t[1]))
            totals = lax.psum((local_sq[0], local_sq[1]), "col")
            inner = lax.psum(local_inner, ("row", "col"))
            sigma = tuple((jnp.sqrt(totals[k] + 1e-06) for k in range(2)))
            right = tuple((prod_t[k] / sigma[k] for k in range(2)))
    results = []
    for k in range(2):
        gain = gain_pair[k]
        outer = left_b[k].astype(jnp.float32)[:, None] * right[k][None, :]
        scaled = gain / sigma[k] * grad_ws[k] - gain * inner[k] / (sigma[k] * sigma[k]) * outer
        results.append(scaled.astype(jnp.bfloat16))
    gain_grads = jnp.stack([inner[0] / sigma[0], inner[1] / sigma[1]])
    return (results[0], results[1], gain_grads, lefts[0], right[0], lefts[1], right[1])


def solution(mesh):
    in_specs = (
        P(),
        P("row", "col"),
        P("row", "col"),
        P("row", "col"),
        P("col", "row"),
        P("row", "col"),
        P("col", "row"),
        P("col"),
        P("col"),
    )
    out_specs = (P("row", "col"), P("row", "col"), P(), P("row"), P("col"), P("row"), P("col"))
    return jax.shard_map(local, mesh=mesh, in_specs=in_specs, out_specs=out_specs, check_vma=False)
```

profile of v0, /device:TPU:0, one launch (start us, length us, event | category | flops | bytes accessed | tf_op | source)
XLA Modules:
  0.0 466.3 jit_solution(9681251987563978492)
XLA Ops:
  11.7 6.5 %fusion.3 = f32[1,3072]{1,0:T(1,128)S(1)} fusion(bf16[3072,1536]{1,0:T(8,128)(2,1)} %param.10, bf16[1536,1]{0,1:T(2,128)(2,1)S(1)} %reshape.18), kind=kOutput, calls=%fused_computation.24 | convolution fusion | flops 9437184 | bytes 9452544 | tf_op jit(solution)/shard_map/dot_general | solution.py:45
  18.2 2.6 convolution_reduce_fusion.3
  20.8 20.5 %all-reduce.7 = (f32[3072]{0:T(1024)S(1)}, f32[768]{0:T(1024)S(1)}) all-reduce(f32[3072]{0:T(1024)S(1)} %bitcast.30, f32[768]{0:T(1024)S(1)} %convolution_reduce_fusion.3), channel_id=1, replica_groups=mesh['row'=8,'col'=4] {'col'}, use_global_device_ids=true, to_apply=%region_0.0 | all-reduce | flops 3840 | bytes 30720 | tf_op jit(solution)/shard_map/psum | solution.py:47
  42.5 12.6 %all-reduce.4 = (f32[]{:T(128)}, f32[]{:T(128)}) all-reduce(f32[]{:T(128)} %multiply_reduce_fusion.4, f32[]{:T(128)} %multiply_reduce_fusion.7), channel_id=1, replica_groups=mesh['row'=8,'col'=4] {'row'}, use_global_device_ids=true, to_apply=%region_2.0 | all-reduce | flops 2 | bytes 16 | tf_op jit(solution)/shard_map/psum | solution.py:48
  56.6 5.3 %fusion.5 = f32[1,6144]{1,0:T(1,128)S(1)} fusion(bf16[768,1]{0,1:T(2,128)(2,1)S(1)} %reshape.28, bf16[768,6144]{1,0:T(8,128)(2,1)} %param.11), kind=kOutput, calls=%fused_computation.26 | convolution fusion | flops 9437184 | bytes 9463296 | tf_op jit(solution)/shard_map/dot_general | solution.py:52
  61.9 5.9 %convolution_reduce_fusion.1 = f32[1536]{0:T(1024)S(1)} fusion(bf16[3072,1]{0,1:T(2,128)(2,1)S(1)} %reshape.20, bf16[3072,1536]{1,0:T(8,128)(2,1)} %param.10), kind=kOutput, calls=%fused_computation.5 | convolution fusion | flops 9437184 | bytes 9449472 | tf_op jit(solution)/shard_map/dot_general | solution.py:52
  67.8 24.1 %all-reduce.3 = (bf16[1536]{0:T(1024)(128)(2,1)S(1)}, bf16[6144]{0:T(1024)(128)(2,1)S(1)}) all-reduce(f32[1536]{0:T(1024)S(1)} %convolution_reduce_fusion.1, f32[6144]{0:T(1024)S(1)} %bitcast.28), channel_id=1, replica_groups=mesh['row'=8,'col'=4] {'row'}, use_global_device_ids=true, to_apply=%region_3.0 | all-reduce | flops 7680 | bytes 46080 | tf_op jit(solution)/shard_map/psum | solution.py:54
  92.0 6.2 %fusion.4 = f32[1,3072]{1,0:T(1,128)S(1)} fusion(bf16[1536,1]{0,1:T(2,128)(2,1)S(1)} %reshape.22, bf16[3072,1536]{1,0:T(8,128)(2,1)} %param.10), kind=kOutput, calls=%fused_computation.25 | convolution fusion | flops 9437184 | bytes 9452544 | tf_op jit(solution)/shard_map/dot_general | solution.py:45
  98.2 6.3 %convolution_reduce_fusion.2 = f32[768]{0:T(1024)S(1)} fusion(bf16[6144,1]{0,1:T(2,128)(2,1)S(1)} %reshape.30, bf16[768,6144]{1,0:T(8,128)(2,1)} %param.11), kind=kOutput, calls=%fused_computation.6 | convolution fusion | flops 9437184 | bytes 9452544 | tf_op jit(solution)/shard_map/dot_general | solution.py:45
  104.5 17.6 %all-reduce.6 = (f32[3072]{0:T(1024)S(1)}, f32[768]{0:T(1024)S(1)}) all-reduce(f32[3072]{0:T(1024)S(1)} %bitcast.31, f32[768]{0:T(1024)S(1)} %convolution_reduce_fusion.2), channel_id=1, replica_groups=mesh['row'=8,'col'=4] {'col'}, use_global_device_ids=true, to_apply=%region_4.0 | all-reduce | flops 3840 | bytes 30720 | tf_op jit(solution)/shard_map/psum | solution.py:47
  123.4 14.0 %all-reduce.2 = (f32[]{:T(128)}, f32[]{:T(128)}) all-reduce(f32[]{:T(128)} %multiply_reduce_fusion.3, f32[]{:T(128)} %multiply_reduce_fusion.6), channel_id=1, replica_groups=mesh['row'=8,'col'=4] {'row'}, use_global_device_ids=true, to_apply=%region_6.0 | all-reduce | flops 2 | bytes 16 | tf_op jit(solution)/shard_map/psum | solution.py:48
  140.0 5.0 %fusion.6 = f32[1,6144]{1,0:T(1,128)S(1)} fusion(bf16[768,1]{0,1:T(2,128)(2,1)S(1)} %reshape.32, bf16[768,6144]{1,0:T(8,128)(2,1)} %param.11), kind=kOutput, calls=%fused_computation.27 | convolution fusion | flops 9437184 | bytes 9463296 | tf_op jit(solution)/shard_map/dot_general | solution.py:52
  145.0 5.1 %convolution_reduce_fusion = f32[1536]{0:T(1024)S(1)} fusion(bf16[3072,1]{0,1:T(2,128)(2,1)S(1)} %reshape.24, bf16[3072,1536]{1,0:T(8,128)(2,1)} %param.10), kind=kOutput, calls=%fused_computation.4 | convolution fusion | flops 9437184 | bytes 9449472 | tf_op jit(solution)/shard_map/dot_general | solution.py:52
  150.1 24.2 %all-reduce.1 = (f32[1536]{0:T(1024)S(1)}, f32[6144]{0:T(1024)S(1)}) all-reduce(f32[1536]{0:T(1024)S(1)} %convolution_reduce_fusion, f32[6144]{0:T(1024)S(1)} %bitcast.29), channel_id=1, replica_groups=mesh['row'=8,'col'=4] {'row'}, use_global_device_ids=true, to_apply=%region_7.0 | all-reduce | flops 7680 | bytes 61440 | tf_op jit(solution)/shard_map/psum | solution.py:54
  175.5 22.2 %all-reduce.5 = (f32[]{:T(128)}, f32[]{:T(128)}) all-reduce(f32[]{:T(128)} %multiply_reduce_fusion.5, f32[]{:T(128)} %multiply_reduce_fusion.2), channel_id=1, replica_groups=mesh['row'=8,'col'=4] {'col'}, use_global_device_ids=true, to_apply=%region_9.0 | all-reduce | flops 2 | bytes 16 | tf_op jit(solution)/shard_map/psum | solution.py:59
  201.1 19.7 %all-gather.5.cloned.1.call-done = bf16[1536,3072]{1,0:T(8,128)(2,1)} async-done(((bf16[384,3072]{1,0:T(8,128)(2,1)}), bf16[1536,3072]{1,0:T(8,128)(2,1)}) %all-gather.5.cloned.1.call-update) | async-done | bytes 9437200 | tf_op jit(solution)/shard_map/all_gather | solution.py:33
  220.8 24.4 %multiply_reduce_fusion.1 = (f32[]{:T(128)}, f32[3072,1536]{1,0:T(8,128)}) fusion(bf16[3072,1536]{1,0:T(8,128)(2,1)} %param.10, bf16[1536,3072]{1,0:T(8,128)(2,1)} %all-gather.5.cloned.1.call-done, bf16[1536,1536]{1,0:T(8,128)(2,1)} %all-gather.7.cloned.1.call-done), kind=kOutput, calls=%fused_computation.3 | convolution fusion | flops 14509670400 | bytes 42467332 | tf_op jit(solution)/shard_map/dot_general | solution.py:10
  245.2 25.9 %all-gather.9.cloned.1.call-done = bf16[1536,768]{1,0:T(8,128)(2,1)} async-done(((bf16[384,768]{1,0:T(8,128)(2,1)}), bf16[1536,768]{1,0:T(8,128)(2,1)}) %all-gather.9.cloned.1.call-update) | async-done | bytes 2359312 | tf_op jit(solution)/shard_map/all_gather | solution.py:34
  271.2 99.3 %all-gather.11.cloned.1.call-done = bf16[1536,6144]{1,0:T(8,128)(2,1)} async-done(((bf16[192,6144]{1,0:T(8,128)(2,1)}), bf16[1536,6144]{1,0:T(8,128)(2,1)}) %all-gather.11.cloned.1.call-update) | async-done | bytes 18874384 | tf_op jit(solution)/shard_map/all_gather | solution.py:29
  370.5 24.8 %multiply_reduce_fusion = (f32[]{:T(128)}, f32[768,6144]{1,0:T(8,128)}) fusion(bf16[768,6144]{1,0:T(8,128)(2,1)} %param.11, bf16[1536,768]{1,0:T(8,128)(2,1)} %all-gather.9.cloned.1.call-done, bf16[1536,6144]{1,0:T(8,128)(2,1)} %all-gather.11.cloned.1.call-done), kind=kOutput, calls=%fused_computation.1 | convolution fusion | flops 14509670400 | bytes 49545220 | tf_op jit(solution)/shard_map/dot_general | solution.py:10
  395.2 39.6 %all-reduce = (f32[]{:T(128)}, f32[]{:T(128)}) all-reduce(f32[]{:T(128)} %get-tuple-element.31, f32[]{:T(128)} %get-tuple-element.33), channel_id=1, replica_groups=mesh['row'=8,'col'=4] {'row','col'}, use_global_device_ids=true, to_apply=%region_11.0 | all-reduce | flops 2 | bytes 16 | tf_op jit(solution)/shard_map/psum | solution.py:60
  439.4 13.0 %subtract_convert_fusion.1 = bf16[3072,1536]{1,0:T(8,128)(2,1)} fusion(f32[3072,1536]{1,0:T(8,128)} %get-tuple-element.32, f32[1536]{0:T(1024)S(1)} %broadcast_divide_fusion.2, f32[3072]{0:T(1024)S(1)} %get-tuple-element.26, f32[]{:T(128)S(6)} %div.59, f32[]{:T(128)S(6)} %div.58), kind=kLoop, calls=%fused_computation.2 | loop fusion | flops 23592960 | bytes 28329992 | tf_op jit(solution)/shard_map/convert_element_type | solution.py:68
  452.4 2.2 copy-done.1
  454.6 5.2 %subtract_convert_fusion = bf16[768,6144]{1,0:T(8,128)(2,1)} fusion(f32[768,6144]{1,0:T(8,128)S(1)} %copy-done.1, f32[6144]{0:T(1024)S(1)} %broadcast_divide_fusion, f32[768]{0:T(1024)S(1)} %get-tuple-element.23, f32[]{:T(128)S(6)} %div.67, f32[]{:T(128)S(6)} %div.66), kind=kLoop, calls=%fused_computation | loop fusion | flops 23592960 | bytes 28339208 | tf_op jit(solution)/shard_map/convert_element_type | solution.py:68
  (42 shorter events, 10.6 us)
Async XLA Ops:
  7.2 193.9 %all-gather.7.cloned.1.call-start = ((), (), s32[]{:S(2)}) async-start(), calls=%async_computation.1 | async-start | bytes 5308416 | tf_op jit(solution)/shard_map/all_gather | solution.py:28
  7.9 212.9 %all-gather.5.cloned.1.call-start = ((), (), s32[]{:S(2)}) async-start(), calls=%async_computation | async-start | bytes 11796480 | tf_op jit(solution)/shard_map/all_gather | solution.py:33
  8.6 262.5 %all-gather.9.cloned.1.call-start = ((), (), s32[]{:S(2)}) async-start(), calls=%async_computation.2 | async-start | bytes 2949120 | tf_op jit(solution)/shard_map/all_gather | solution.py:34
  9.4 361.1 %all-gather.11.cloned.1.call-start = ((), (), s32[]{:S(2)}) async-start(), calls=%async_computation.3 | async-start | bytes 21233664 | tf_op jit(solution)/shard_map/all_gather | solution.py:29
  10.0 8.3 %copy-start = (bf16[768,6144]{1,0:T(8,128)(2,1)S(1)}, bf16[768,6144]{1,0:T(8,128)(2,1)}, u32[]{:S(2)}) copy-start(bf16[768,6144]{1,0:T(8,128)(2,1)} %param.11) | copy-start | bytes 28311556
  145.0 53.4 %copy-start.4 = (f32[2]{0:T(128)S(1)}, f32[2]{0:T(128)}, u32[]{:S(2)}) copy-start(f32[2]{0:T(128)} %param.9) | copy-start | bytes 28
  201.1 238.3 %copy-start.3 = (f32[1536]{0:T(1024)}, f32[1536]{0:T(1024)S(1)}, u32[]{:S(2)}) copy-start(f32[1536]{0:T(1024)S(1)} %broadcast_divide_fusion.2) | copy-start | bytes 18436
  201.1 251.3 %copy-start.2 = (f32[6144]{0:T(1024)}, f32[6144]{0:T(1024)S(1)}, u32[]{:S(2)}) copy-start(f32[6144]{0:T(1024)S(1)} %broadcast_divide_fusion) | copy-start | bytes 73732
  439.4 15.2 %copy-start.1 = (f32[768,6144]{1,0:T(8,128)S(1)}, f32[768,6144]{1,0:T(8,128)}, u32[]{:S(2)}) copy-start(f32[768,6144]{1,0:T(8,128)} %get-tuple-element.34) | copy-start | bytes 56623108
Sparse Core Ops, SparseCore 0:
  9.9 41.6 all-gather.6
  53.2 167.5 all-gather.4
  222.4 48.7 all-gather.8
  272.9 97.5 all-gather.10
where the time goes:
time: 467 us; the launch traced here: 466 us
  blocking collectives  175 us (37%)
  waiting for transfers between devices  148 us (32%)
  matrix products  92.2 us (20%)
  other arithmetic  25.4 us (5%)
  between operations  23.3 us (5%)
    all_gather x1, waiting for transfers between devices, local(): lax.all_gather(inputs_down, 'row', axis=0, tiled=True)  99.3 us
    dot_general x2, matrix products, contract(): lax.dot_general(first, second, (((0,), (0,)), ((), ())), preferred_elemen...  49.2 us
    psum x2, blocking collectives, local(): prod_t = lax.psum(partial_t, 'row')  48.3 us
    psum x1, blocking collectives, local(): inner = lax.psum(local_inner, ('row', 'col'))  39.6 us
    psum x2, blocking collectives, local(): prod_s = lax.psum(partial_s, 'col')  38.1 us
    psum x2, blocking collectives, local(): lax.psum((jnp.sum(prod_s[0] * prod_s[0]), jnp.sum(prod_s[1] * prod_s[1]))...  26.6 us
    all_gather x1, waiting for transfers between devices, local(): lax.all_gather(grads_down, 'col', axis=0, tiled=True)  25.9 us
    psum x1, blocking collectives, local(): totals = lax.psum((local_sq[0], local_sq[1]), 'col')  22.2 us
  transfers between devices with their start and end apart: 4, of which 3 were waited for; matrix products, arithmetic and copies ran while one was open for 16% of the time, Pallas kernels for 0%

commit v1 on v0

v1 whole, which is shorter than its diff:
```python
import functools

import jax
import jax.numpy as jnp
from jax import lax
from jax.experimental import pallas as pl
from jax.experimental.pallas import tpu as pltpu
from jax.sharding import PartitionSpec as P

EPS = 1e-06
LANES = 128
PARAMS = pltpu.CompilerParams(vmem_limit_bytes=56 * 1024 * 1024)
F32 = jnp.float32
BF16 = jnp.bfloat16


def all_sum(value, axis, size):
    step = 1
    while step < size:
        value = value + lax.ppermute(value, axis, [(i, i ^ step) for i in range(size)])
        step *= 2
    return value


def exchange(value, axis, size):
    return [value] + [
        lax.ppermute(value, axis, [(i, i ^ k) for i in range(size)]) for k in range(1, size)
    ]


def tree(terms):
    while len(terms) > 1:
        terms = [terms[i] + terms[i + 1] for i in range(0, len(terms), 2)]
    return terms[0]


def fence(*values):
    return lax.optimization_barrier(values)


def tile_of(extent, most):
    tile = min(extent, most)
    while extent % tile:
        tile -= LANES
    return tile


def column_of(row):
    return jnp.broadcast_to(row, (LANES, row.shape[1])).T


def row_of(block):
    return jnp.sum(block.T, axis=0, keepdims=True)


def norm_of(squares):
    return jnp.sqrt(jnp.sum(squares, axis=1, keepdims=True) + EPS)


def whole(array):
    return pl.BlockSpec(array.shape, lambda *_: (0,) * array.ndim)


def row_blocks(weights):
    steps = weights[1].shape[0] // LANES
    return [w.shape[0] // steps for w in weights], steps


def left_product(rights, weights):
    heights, steps = row_blocks(weights)
    extents = [w.shape[0] for w in weights]

    def kernel(v_up_ref, v_down_ref, w_up_ref, w_down_ref, out_ref):
        step = pl.program_id(0)
        offset = 0
        for k, (w_ref, v_ref) in enumerate(((w_up_ref, v_up_ref), (w_down_ref, v_down_ref))):
            height, depth = w_ref.shape
            sums = []
            for top in range(0, height, 64):
                total = jnp.zeros((64, LANES), F32)
                for c in range(0, depth, LANES):
                    v = v_ref[:, c : c + LANES].astype(BF16).astype(F32)
                    total += w_ref[top : top + 64, c : c + LANES].astype(F32) * v
                sums.append(total)
            start = pl.multiple_of(offset + step * height, LANES)
            out_ref[:, pl.ds(start, height)] = row_of(jnp.concatenate(sums))
            offset += extents[k]

    return pl.pallas_call(
        kernel,
        grid=(steps,),
        in_specs=[whole(r) for r in rights]
        + [pl.BlockSpec((heights[k], weights[k].shape[1]), lambda i: (i, 0)) for k in range(2)],
        out_specs=pl.BlockSpec((1, sum(extents)), lambda i: (0, 0)),
        out_shape=jax.ShapeDtypeStruct((1, sum(extents)), F32),
        compiler_params=PARAMS,
    )(*rights, *weights)


def right_product(terms, weights):
    heights, steps = row_blocks(weights)
    extents = [w.shape[0] for w in weights]
    spans = [w.shape[1] for w in weights]
    count = len(terms)

    def kernel(*refs):
        w_refs, (left_ref, out_ref) = refs[count : count + 2], refs[count + 2 :]
        step = pl.program_id(0)

        @pl.when(step == 0)
        def _():
            out_ref[...] = jnp.zeros_like(out_ref)
            left_ref[...] = tree([ref[...] for ref in refs[:count]])

        row = lane = 0
        for k in range(2):
            start = pl.multiple_of(row + step * heights[k], LANES)
            left = left_ref[:, pl.ds(start, heights[k])]
            column = column_of(left.astype(BF16).astype(F32))
            for c in range(0, spans[k], LANES):
                total = jnp.zeros((8, LANES), F32)
                for top in range(0, heights[k], 64):
                    product = w_refs[k][top : top + 64, c : c + LANES].astype(F32) * column[top : top + 64]
                    total += jnp.sum(product.reshape(8, 8, LANES), axis=0)
                out_ref[:, lane + c : lane + c + LANES] += jnp.sum(total, axis=0, keepdims=True)
            squares = left * left
            here = slice(sum(spans) + k * LANES, sum(spans) + (k + 1) * LANES)
            for c in range(0, heights[k], LANES):
                out_ref[:, here] += squares[:, c : c + LANES]
            row += extents[k]
            lane += spans[k]

    total = sum(spans) + 2 * LANES
    return pl.pallas_call(
        kernel,
        grid=(steps,),
        in_specs=[whole(t) for t in terms]
        + [pl.BlockSpec((heights[k], spans[k]), lambda i: (i, 0)) for k in range(2)],
        out_specs=[pl.BlockSpec((1, sum(extents)), lambda i: (0, 0)), pl.BlockSpec((1, total), lambda i: (0, 0))],
        out_shape=[jax.ShapeDtypeStruct((1, sum(extents)), F32), jax.ShapeDtypeStruct((1, total), F32)],
        compiler_params=PARAMS,
    )(*terms, *weights)


def scale_right(total, spans):
    def kernel(total_ref, up_ref, down_ref, squares_ref):
        lane = 0
        for k, ref in enumerate((up_ref, down_ref)):
            here = sum(spans) + k * LANES
            ref[...] = total_ref[:, lane : lane + spans[k]] / norm_of(total_ref[:, here : here + LANES])
            squares = jnp.zeros((1, LANES), F32)
            for c in range(0, spans[k], LANES):
                squares += ref[:, c : c + LANES] * ref[:, c : c + LANES]
            squares_ref[k : k + 1, :] = squares
            lane += spans[k]

    return pl.pallas_call(
        kernel,
        out_shape=[jax.ShapeDtypeStruct((1, span), F32) for span in spans]
        + [jax.ShapeDtypeStruct((2, LANES), F32)],
        compiler_params=PARAMS,
    )(total)


def grad_chunk(order, blocks, inputs, weight, chunk, buffer, inner, which):
    count = len(blocks)
    tokens, width = blocks[0].shape
    depth, columns = inputs.shape
    tile = tile_of(columns, 512)

    def kernel(order_ref, *refs):
        x_ref, w_ref, before_ref = refs[count : count + 3]
        g_ref, inner_ref, turned = refs[-3:]

        @pl.when(pl.program_id(0) == 0)
        def _():
            inner_ref[...] = before_ref[...]
            for slot in range(count):
                start = pl.multiple_of(order_ref[slot] * tokens, LANES)
                turned[:, pl.ds(start, tokens)] = refs[slot][...].T

        here = slice(8 * which, 8 * which + 8)
        total = jnp.dot(turned[...], x_ref[...], preferred_element_type=F32)
        g_ref[...] = total.astype(g_ref.dtype)
        product = total * w_ref[...].astype(F32)
        product = jnp.sum(product.reshape(-1, 8, tile), axis=0)
        inner_ref[here, :] += sum(product[:, c : c + LANES] for c in range(0, tile, LANES))

    in_specs = [pl.BlockSpec((tokens, width), lambda j, o: (0, 0)) for _ in blocks]
    in_specs += [
        pl.BlockSpec((depth, tile), lambda j, o: (0, j)),
        pl.BlockSpec((width, tile), lambda j, o: (chunk, j)),
        pl.BlockSpec((16, LANES), lambda j, o: (0, 0)),
    ]
    operands = [order, *blocks, inputs, weight, inner]
    aliases = {}
    if buffer is not None:
        in_specs.append(pl.BlockSpec(memory_space=pl.ANY))
        operands.append(buffer)
        aliases = {count + 4: 0}
    return pl.pallas_call(
        kernel,
        grid_spec=pltpu.PrefetchScalarGridSpec(
            num_scalar_prefetch=1,
            grid=(columns // tile,),
            in_specs=in_specs,
            out_specs=[
                pl.BlockSpec((width, tile), lambda j, o: (chunk, j)),
                pl.BlockSpec((16, LANES), lambda j, o: (0, 0)),
            ],
            scratch_shapes=[pltpu.VMEM((width, depth), BF16)],
        ),
        out_shape=[
            jax.ShapeDtypeStruct(weight.shape, BF16),
            jax.ShapeDtypeStruct((16, LANES), F32),
        ],
        input_output_aliases=aliases,
        compiler_params=PARAMS,
    )(*operands)


def finish(grads, left, norms, rights, squares, inners, gains):
    heights, steps = row_blocks(grads)
    extents = [g.shape[0] for g in grads]
    spans = [g.shape[1] for g in grads]
    count = len(squares)

    def kernel(left_ref, norms_ref, *refs):
        v_refs, refs = refs[:2], refs[2:]
        square_refs, refs = refs[:count], refs[count:]
        inner_refs, refs = refs[:count], refs[count:]
        gains_ref, refs = refs[0], refs[1:]
        g_refs, out_refs, gain_ref = refs[:2], refs[2:4], refs[4]
        step = pl.program_id(0)
        square = tree([ref[...] for ref in square_refs])
        inner = tree([ref[...] for ref in inner_refs])
        row = 0
        for k in range(2):
            sigma = norm_of(square[k : k + 1])
            gw = jnp.sum(jnp.sum(inner[8 * k : 8 * k + 8], axis=0, keepdims=True), axis=1, keepdims=True)
            gain = gains_ref[k : k + 1, :1]
            scale = gain / sigma
            slope = gain * gw / (sigma * sigma)
            gain_ref[k : k + 1, :] = jnp.broadcast_to(gw / sigma, (1, LANES))
            start = pl.multiple_of(row + step * heights[k], LANES)
            norm = norm_of(norms_ref[:, k * LANES : (k + 1) * LANES])
            column = column_of((left_ref[:, pl.ds(start, heights[k])] / norm).astype(BF16).astype(F32))
            for c in range(0, spans[k], LANES):
                here = slice(c, c + LANES)
                v = slope * (v_refs[k][:, here] / sigma)
                out_refs[k][:, here] = (scale * g_refs[k][:, here].astype(F32) - column * v).astype(BF16)
            row += extents[k]

    operands = [left, norms, *rights, *squares, *inners, gains]
    blocks = [pl.BlockSpec((heights[k], spans[k]), lambda i: (i, 0)) for k in range(2)]
    return pl.pallas_call(
        kernel,
        grid=(steps,),
        in_specs=[whole(o) for o in operands] + blocks,
        out_specs=blocks + [pl.BlockSpec((2, LANES), lambda i: (0, 0))],
        out_shape=[jax.ShapeDtypeStruct(g.shape, BF16) for g in grads] + [jax.ShapeDtypeStruct((2, LANES), F32)],
        compiler_params=PARAMS,
    )(*operands, *grads)


def local(
    rows,
    cols,
    gain_pair,
    weight_up,
    weight_down,
    inputs_up,
    grads_up,
    inputs_down,
    grads_down,
    vector_up,
    vector_down,
):
    weights = (weight_up, weight_down)
    inputs_all = (
        lax.all_gather(inputs_up, "row", axis=0, tiled=True),
        lax.all_gather(inputs_down, "row", axis=0, tiled=True),
    )
    extents = (weight_up.shape[0], weight_down.shape[0])
    spans = (weight_up.shape[1], weight_down.shape[1])
    ring = [(i, (i + 1) % cols) for i in range(cols)]
    order = lax.rem(lax.axis_index("col") - jnp.arange(cols, dtype=jnp.int32) + cols, jnp.int32(cols))
    gains = jnp.broadcast_to(gain_pair[:, None], (2, LANES))

    unit = grads_up.shape[1] // 6
    chunks = [
        [grads_down, grads_up[:, : 2 * unit]],
        [grads_up[:, 2 * unit : 4 * unit]],
        [grads_up[:, 4 * unit : 5 * unit]],
        [grads_up[:, 5 * unit :]],
    ]
    streams = [[chunk] for chunk in chunks]

    def hop(pieces):
        return [lax.ppermute(piece, "col", ring) for piece in pieces]

    def advance(number, *others):
        held, *others = fence(streams[number][-1], *others)
        streams[number][-1] = held
        streams[number].append(hop(held))
        return others

    def land(number, *others):
        held, *others = fence(streams[number][-1], *others)
        streams[number][-1] = held
        return others

    grad_ws = [None, None]
    inner = jnp.zeros((16, LANES), F32)

    def multiply(k, number, place, chunk):
        slots = [pieces[place] for pieces in streams[number]]
        return grad_chunk(order, slots, inputs_all[k], weights[k], chunk, grad_ws[k], inner, k)

    streams[0].append(hop(chunks[0]))
    streams[1].append(hop(chunks[1]))
    part = left_product((vector_up[None, :], vector_down[None, :]), weights)
    terms = exchange(part, "col", cols)
    (terms,) = advance(0, terms)
    (terms,) = advance(1, terms)
    left, total = right_product(terms, weights)
    *rights, _ = scale_right(all_sum(total, "row", rows), spans)
    part = left_product(rights, weights)
    (part,) = advance(0, part)
    terms = exchange(part, "col", cols)
    (terms,) = advance(1, terms)
    left, total = right_product(terms, weights)
    total = all_sum(total, "row", rows)
    for _ in range(cols - 4):
        (total,) = advance(0, total)
        (total,) = advance(1, total)
    (total,) = land(0, total)
    (total,) = advance(2, total)
    *rights, square = scale_right(total, spans)
    squares = exchange(square, "col", cols)
    (inner,) = advance(3, inner)
    grad_ws[0], inner = multiply(0, 0, 1, 0)
    (inner,) = land(1, inner)
    for step in range(cols - 2):
        (inner,) = advance(2, inner)
        if step == 0:
            grad_ws[0], inner = multiply(0, 1, 0, 1)
        (inner,) = advance(3, inner)
    grad_ws[1], inner = multiply(1, 0, 0, 0)
    (inner,) = land(2, inner)
    grad_ws[0], inner = multiply(0, 2, 0, 4)
    (inner,) = land(3, inner)
    grad_ws[0], inner = multiply(0, 3, 0, 5)
    inners = exchange(all_sum(inner, "row", rows), "col", cols)
    norms = total[:, sum(spans) :]
    wgrad_up, wgrad_down, gain_grads = finish(grad_ws, left, norms, rights, squares, inners, gains)

    norm = jnp.sqrt(jnp.sum(norms.reshape(2, LANES), axis=1) + EPS)
    sigma = jnp.sqrt(jnp.sum(tree(squares), axis=1) + EPS)
    left_up = left[0, : extents[0]] / norm[0]
    left_down = left[0, extents[0] :] / norm[1]
    right_up, right_down = (rights[k][0] / sigma[k] for k in range(2))
    return wgrad_up, wgrad_down, gain_grads[:, 0], left_up, right_up, left_down, right_down


def solution(mesh):
    in_specs = (
        P(),
        P("row", "col"),
        P("row", "col"),
        P("row", "col"),
        P("col", "row"),
        P("row", "col"),
        P("col", "row"),
        P("col"),
        P("col"),
    )
    out_specs = (P("row", "col"), P("row", "col"), P(), P("row"), P("col"), P("row"), P("col"))
    body = functools.partial(local, mesh.shape["row"], mesh.shape["col"])
    return jax.shard_map(body, mesh=mesh, in_specs=in_specs, out_specs=out_specs, check_vma=False)
```

time: 467 us -> 297 us (0.64)
  blocking collectives: 175 us -> 0 us
  Pallas kernels: 0 us -> 122 us
  matrix products: 92.2 us -> 0 us
  waiting for transfers between devices: 148 us -> 95.4 us
  starting transfers between devices: 0.15 us -> 44 us
  other arithmetic: 25.4 us -> 10.1 us
  between operations: 23.3 us -> 14.4 us
  local copies, waits for them, and re-layouts: 2.88 us -> 10.3 us
    psum x8 -> x0, blocking collectives: 175 us -> none  [the longest x2 48.3 us: local(): prod_t = lax.psum(partial_t, 'row')]
    pallas_call x0 -> x12, Pallas kernels: none -> 122 us  [the longest x5 61.8 us: grad_chunk(): pl.pallas_call(kernel, grid_spec=pltpu.PrefetchScalarGridSpec(num_scalar_...]
    all_gather x1, waiting for transfers between devices: 99.3 us -> 0.01 us  [local(): lax.all_gather(inputs_down, 'row', axis=0, tiled=True)]
    ppermute x0 -> x36, waiting for transfers between devices: none -> 94 us  [the longest x12 66.8 us: exchange(): lax.ppermute(value, axis, [(i, i ^ k) for i in range(size)])]
    dot_general x10 -> x0, matrix products: 92.2 us -> none  [the longest x2 49.2 us: contract(): lax.dot_general(first, second, (((0,), (0,)), ((), ())), preferred_elemen...]
    all_gather x2 -> x0, waiting for transfers between devices: 45.6 us -> none  [the longest x1 25.9 us: local(): lax.all_gather(grads_down, 'col', axis=0, tiled=True)]
    ppermute x0 -> x36, starting transfers between devices: none -> 43.9 us  [the longest x15 17.7 us: hop(): return [lax.ppermute(piece, 'col', ring) for piece in pieces]]
    convert_element_type x8 -> x0, other arithmetic: 21.2 us -> none  [the longest x2 18.2 us: local(): results.append(scaled.astype(jnp.bfloat16))]
  transfers between devices with their start and end apart: 4 -> 38, of which waited for: 3 -> 17; matrix products, arithmetic and copies ran while one was open for 16% -> 5% of each run, Pallas kernels for 0% -> 33%
where the time goes in v1:
time: 297 us; the launch traced here: 296 us
  Pallas kernels  122 us (41%)
  waiting for transfers between devices  95.4 us (32%)
  starting transfers between devices  44 us (15%)
  between operations  14.4 us (5%)
  local copies, waits for them, and re-layouts  10.3 us (3%)
  other arithmetic  10.1 us (3%)
    ppermute x12, waiting for transfers between devices, exchange(): lax.ppermute(value, axis, [(i, i ^ k) for i in range(size)])  66.8 us
    pallas_call x5, Pallas kernels, grad_chunk(): pl.pallas_call(kernel, grid_spec=pltpu.PrefetchScalarGridSpec(num_scalar_...  61.8 us
    pallas_call x2, Pallas kernels, left_product(): pl.pallas_call(kernel, grid=(steps,), in_specs=[whole(r) for r in rights]...  21.7 us
    pallas_call x2, Pallas kernels, right_product(): pl.pallas_call(kernel, grid=(steps,), in_specs=[whole(t) for t in terms]...  20.1 us
    ppermute x15, starting transfers between devices, hop(): return [lax.ppermute(piece, 'col', ring) for piece in pieces]  17.7 us
    ppermute x12, starting transfers between devices, exchange(): lax.ppermute(value, axis, [(i, i ^ k) for i in range(size)])  17.6 us
    ppermute x9, waiting for transfers between devices, all_sum(): lax.ppermute(value, axis, [(i, i ^ step) for i in range(size)])  16.6 us
    pallas_call x1, Pallas kernels, finish(): pl.pallas_call(kernel, grid=(steps,), in_specs=[whole(o) for o in operand...  15.3 us
  transfers between devices with their start and end apart: 38, of which 17 were waited for; matrix products, arithmetic and copies ran while one was open for 5% of the time, Pallas kernels for 33%

profile of v1, /device:TPU:0, one launch (start us, length us, event | category | flops | bytes accessed | tf_op | source)
XLA Modules:
  0.0 296.0 jit_solution(3316451743405761831)
XLA Ops:
  10.2 3.1 %collective-permute-start.2 = (bf16[384,1024]{1,0:T(8,128)(2,1)S(1)}, bf16[384,1024]{1,0:T(8,128)(2,1)S(1)}, u32[]{:S(2)}, u32[]{:S(2)}) collective-permute-start(bf16[384,1024]{1,0:T(8,128)(2,1)S(1)} %get-tuple-element.131.refs_0_), channel_id=1, source_target_pairs={{0,1},{1,2},{2,3},{3,0},{4,5},{5,6},{6,7},{7,4},{8,9},{9,10},{10,1... | collective-permute-start | bytes 2359304 | tf_op jit(solution)/shard_map/ppermute | solution.py:300
  17.7 10.2 %shard_map.144.refs_0_ = f32[1,3840]{1,0:T(1,128)} custom-call(f32[1,1536]{1,0:T(1,128)} %broadcast_in_dim.15.v_up_ref, f32[1,6144]{1,0:T(1,128)} %bitcast.8, bf16[3072,1536]{1,0:T(8,128)(2,1)} %refs_5_.13, bf16[768,6144]{1,0:T(8,128)(2,1)} %refs_5_.11), custom_call_target="tpu_custom_call" | custom-call | tf_op jit(solution)/shard_map/pallas_call | solution.py:89
  28.0 2.7 collective-permute-start.4
  30.8 32.2 %collective-permute-done.3.refs_1_ = f32[1,3840]{1,0:T(1,128)S(1)} collective-permute-done((f32[1,3840]{1,0:T(1,128)}, f32[1,3840]{1,0:T(1,128)S(1)}, u32[]{:S(2)}, u32[]{:S(2)}) %collective-permute-start.3) | collective-permute-done | bytes 15392 | tf_op jit(solution)/shard_map/ppermute | solution.py:27
  64.7 4.0 %collective-permute-done.5.refs_3_ = f32[1,3840]{1,0:T(1,128)S(1)} collective-permute-done((f32[1,3840]{1,0:T(1,128)}, f32[1,3840]{1,0:T(1,128)S(1)}, u32[]{:S(2)}, u32[]{:S(2)}) %collective-permute-start.5) | collective-permute-done | bytes 15392 | tf_op jit(solution)/shard_map/ppermute | solution.py:27
  68.9 2.9 collective-permute-start.6
  71.8 10.0 %shard_map.145 = (f32[1,3840]{1,0:T(1,128)}, f32[1,7936]{1,0:T(1,128)}) custom-call(f32[1,3840]{1,0:T(1,128)} %shard_map.144.refs_0_, f32[1,3840]{1,0:T(1,128)} %copy-done.22, f32[1,3840]{1,0:T(1,128)} %copy-done.23, f32[1,3840]{1,0:T(1,128)} %copy-done.24, bf16[3072,1536]{1,0:T(8,128)(2,1)} %refs_5_.13, bf16[768,6144]{1,0:T(8,128)(2,1)} %refs_5_.11), custom_call_target="tpu_custom_call" | custom-call | tf_op jit(solution)/shard_map/pallas_call | solution.py:134
  85.6 3.1 %collective-permute-done.10 = f32[1,7936]{1,0:T(1,128)S(1)} collective-permute-done((f32[1,7936]{1,0:T(1,128)S(1)}, f32[1,7936]{1,0:T(1,128)S(1)}, u32[]{:S(2)}, u32[]{:S(2)}) %collective-permute-start.10) | collective-permute-done | bytes 31776 | tf_op jit(solution)/shard_map/ppermute | solution.py:20
  90.3 2.4 collective-permute-done.11
  94.8 11.5 %shard_map.147.refs_0_ = f32[1,3840]{1,0:T(1,128)} custom-call(f32[1,1536]{1,0:T(1,128)} %get-tuple-element.80.v_up_ref, f32[1,6144]{1,0:T(1,128)} %get-tuple-element.81.v_down_ref, bf16[3072,1536]{1,0:T(8,128)(2,1)} %refs_5_.13, bf16[768,6144]{1,0:T(8,128)(2,1)} %refs_5_.11), custom_call_target="tpu_custom_call" | custom-call | tf_op jit(solution)/shard_map/pallas_call | solution.py:89
  109.3 3.5 %collective-permute-start.13 = (f32[1,3840]{1,0:T(1,128)}, f32[1,3840]{1,0:T(1,128)S(1)}, u32[]{:S(2)}, u32[]{:S(2)}) collective-permute-start(f32[1,3840]{1,0:T(1,128)} %shard_map.147.refs_0_), channel_id=1, source_target_pairs={{0,2},{1,3},{2,0},{3,1},{4,6},{5,7},{6,4},{7,5},{8,10},{9,11},{10,... | collective-permute-start | bytes 46088 | tf_op jit(solution)/shard_map/ppermute | solution.py:27
  112.8 8.0 %collective-permute-done.6.refs_2_ = bf16[384,1024]{1,0:T(8,128)(2,1)S(1)} collective-permute-done((bf16[384,1024]{1,0:T(8,128)(2,1)S(1)}, bf16[384,1024]{1,0:T(8,128)(2,1)S(1)}, u32[]{:S(2)}, u32[]{:S(2)}) %collective-permute-start.6) | collective-permute-done | bytes 786464 | tf_op jit(solution)/shard_map/ppermute | solution.py:300
  120.8 27.5 %collective-permute-done.12.refs_1_ = f32[1,3840]{1,0:T(1,128)S(1)} collective-permute-done((f32[1,3840]{1,0:T(1,128)}, f32[1,3840]{1,0:T(1,128)S(1)}, u32[]{:S(2)}, u32[]{:S(2)}) %collective-permute-start.12) | collective-permute-done | bytes 15392 | tf_op jit(solution)/shard_map/ppermute | solution.py:27
  149.4 10.2 %shard_map.148 = (f32[1,3840]{1,0:T(1,128)}, f32[1,7936]{1,0:T(1,128)}) custom-call(f32[1,3840]{1,0:T(1,128)} %shard_map.147.refs_0_, f32[1,3840]{1,0:T(1,128)} %copy-done.25, f32[1,3840]{1,0:T(1,128)} %copy-done.26, f32[1,3840]{1,0:T(1,128)} %copy-done.27, bf16[3072,1536]{1,0:T(8,128)(2,1)} %refs_5_.13, bf16[768,6144]{1,0:T(8,128)(2,1)} %refs_5_.11), custom_call_target="tpu_custom_call" | custom-call | tf_op jit(solution)/shard_map/pallas_call | solution.py:134
  163.1 2.7 collective-permute-done.18
  172.8 10.9 %shard_map.150 = (bf16[3072,1536]{1,0:T(8,128)(2,1)}, f32[16,128]{1,0:T(8,128)}) custom-call(s32[4]{0:T(128)} %compare_select_fusion.order_ref, bf16[384,1024]{1,0:T(8,128)(2,1)} %copy-done.1, bf16[384,1024]{1,0:T(8,128)(2,1)} %copy-done.5, bf16[384,1024]{1,0:T(8,128)(2,1)} %copy-done.7, bf16[384,1024]{1,0:T(8,128)(2,1)} %copy-done.8, ...), custom_call_target="tpu_custom_call" | custom-call | tf_op jit(solution)/shard_map/pallas_call | solution.py:201
  184.5 2.4 collective-permute-start.27
  186.9 11.0 %shard_map.151 = (bf16[3072,1536]{1,0:T(8,128)(2,1)}, f32[16,128]{1,0:T(8,128)}) custom-call(s32[4]{0:T(128)} %compare_select_fusion.order_ref, bf16[384,1024]{1,0:T(8,128)(2,1)} %copy-done, bf16[384,1024]{1,0:T(8,128)(2,1)} %copy-done.4, bf16[384,1024]{1,0:T(8,128)(2,1)} %copy-done.6, bf16[384,1024]{1,0:T(8,128)(2,1)} %copy-done.9, ...), custom_call_target="tpu_custom_call", output_to_operand_aliasing={{0}: (8, {})} | custom-call | tf_op jit(solution)/shard_map/pallas_call | solution.py:201
  201.0 2.8 collective-permute-start.21
  212.3 24.4 %shard_map.152 = (bf16[768,6144]{1,0:T(8,128)(2,1)}, f32[16,128]{1,0:T(8,128)}) custom-call(s32[4]{0:T(128)} %compare_select_fusion.order_ref, bf16[384,768]{1,0:T(8,128)(2,1)} %refs_0_.1, bf16[384,768]{1,0:T(8,128)(2,1)} %copy-done.10, bf16[384,768]{1,0:T(8,128)(2,1)} %copy-done.11, bf16[384,768]{1,0:T(8,128)(2,1)} %copy-done.12, ...), custom_call_target="tpu_custom_call" | custom-call | tf_op jit(solution)/shard_map/pallas_call | solution.py:201
  237.5 7.7 %shard_map.153 = (bf16[3072,1536]{1,0:T(8,128)(2,1)}, f32[16,128]{1,0:T(8,128)}) custom-call(s32[4]{0:T(128)} %compare_select_fusion.order_ref, bf16[384,512]{1,0:T(8,128)(2,1)} %copy-done.3, bf16[384,512]{1,0:T(8,128)(2,1)} %collective-permute-done.25.refs_1_, bf16[384,512]{1,0:T(8,128)(2,1)} %copy-done.14, ...), custom_call_target="tpu_custom_call", output_to_operand_aliasing={{0}: (8, {})} | custom-call | tf_op jit(solution)/shard_map/pallas_call | solution.py:201
  245.9 7.8 %shard_map.154 = (bf16[3072,1536]{1,0:T(8,128)(2,1)}, f32[16,128]{1,0:T(8,128)}) custom-call(s32[4]{0:T(128)} %compare_select_fusion.order_ref, bf16[384,512]{1,0:T(8,128)(2,1)} %copy-done.2, bf16[384,512]{1,0:T(8,128)(2,1)} %copy-done.13, bf16[384,512]{1,0:T(8,128)(2,1)} %copy-done.15, ...), custom_call_target="tpu_custom_call", output_to_operand_aliasing={{0}: (8, {})} | custom-call | tf_op jit(solution)/shard_map/pallas_call | solution.py:201
  269.2 2.8 collective-permute-done.35.refs_9_
  272.6 15.3 %shard_map.155 = (bf16[3072,1536]{1,0:T(8,128)(2,1)}, bf16[768,6144]{1,0:T(8,128)(2,1)}, f32[2,128]{1,0:T(2,128)}) custom-call(f32[1,3840]{1,0:T(1,128)} %get-tuple-element.87.left_ref, f32[1,256]{1,0:T(1,128)} %copy-done.28, f32[1,1536]{1,0:T(1,128)} %get-tuple-element.93.refs_0_, f32[1,6144]{1,0:T(1,128)} %get-tuple-element.94.refs_1_, ...), custom_call_target="tpu_custom_call" | custom-call | tf_op jit(solution)/shard_map/pallas_call | solution.py:256
  (165 shorter events, 62.6 us)
Async XLA Ops:
  7.2 165.0 %all-gather.3.cloned.1.call-start = ((), (), s32[]{:S(2)}) async-start(), calls=%async_computation | async-start | bytes 5308416 | tf_op jit(solution)/shard_map/all_gather | solution.py:281
  7.9 204.3 %all-gather.5.cloned.1.call-start = ((), (), s32[]{:S(2)}) async-start(), calls=%async_computation.1 | async-start | bytes 21233664 | tf_op jit(solution)/shard_map/all_gather | solution.py:282
  10.2 58.5 %collective-permute-start.2 = (bf16[384,1024]{1,0:T(8,128)(2,1)S(1)}, bf16[384,1024]{1,0:T(8,128)(2,1)S(1)}, u32[]{:S(2)}, u32[]{:S(2)}) collective-permute-start(bf16[384,1024]{1,0:T(8,128)(2,1)S(1)} %get-tuple-element.131.refs_0_), channel_id=1, source_target_pairs={{0,1},{1,2},{2,3},{3,0},{4,5},{5,6},{6,7},{7,4},{8,9},{9,10},{10,1... | collective-permute-start | bytes 2359304 | tf_op jit(solution)/shard_map/ppermute | solution.py:300
  13.2 55.5 %collective-permute-start.1 = (bf16[384,768]{1,0:T(8,128)(2,1)}, bf16[384,768]{1,0:T(8,128)(2,1)S(1)}, u32[]{:S(2)}, u32[]{:S(2)}) collective-permute-start(bf16[384,768]{1,0:T(8,128)(2,1)} %refs_0_.1), channel_id=1, source_target_pairs={{0,1},{1,2},{2,3},{3,0},{4,5},{5,6},{6,7},{7,4},{8,9},{9,10},{10,1... | collective-permute-start | bytes 1769480 | tf_op jit(solution)/shard_map/ppermute | solution.py:300
  14.8 54.0 %collective-permute-start = (bf16[384,1024]{1,0:T(8,128)(2,1)S(1)}, bf16[384,1024]{1,0:T(8,128)(2,1)S(1)}, u32[]{:S(2)}, u32[]{:S(2)}) collective-permute-start(bf16[384,1024]{1,0:T(8,128)(2,1)S(1)} %get-tuple-element.132.refs_0_), channel_id=1, source_target_pairs={{0,1},{1,2},{2,3},{3,0},{4,5},{5,6},{6,7},{7,4},{8,9},{9,10},{10,1... | collective-permute-start | bytes 2359304 | tf_op jit(solution)/shard_map/ppermute | solution.py:300
  27.9 35.0 %collective-permute-start.3 = (f32[1,3840]{1,0:T(1,128)}, f32[1,3840]{1,0:T(1,128)S(1)}, u32[]{:S(2)}, u32[]{:S(2)}) collective-permute-start(f32[1,3840]{1,0:T(1,128)} %shard_map.144.refs_0_), channel_id=1, source_target_pairs={{0,1},{1,0},{2,3},{3,2},{4,5},{5,4},{6,7},{7,6},{8,9},{9,8},{10,11... | collective-permute-start | bytes 46088 | tf_op jit(solution)/shard_map/ppermute | solution.py:27
  28.0 36.7 %collective-permute-start.4 = (f32[1,3840]{1,0:T(1,128)}, f32[1,3840]{1,0:T(1,128)S(1)}, u32[]{:S(2)}, u32[]{:S(2)}) collective-permute-start(f32[1,3840]{1,0:T(1,128)} %shard_map.144.refs_0_), channel_id=1, source_target_pairs={{0,2},{1,3},{2,0},{3,1},{4,6},{5,7},{6,4},{7,5},{8,10},{9,11},{10,... | collective-permute-start | bytes 46088 | tf_op jit(solution)/shard_map/ppermute | solution.py:27
  68.7 37.6 %collective-permute-start.8 = (bf16[384,1024]{1,0:T(8,128)(2,1)S(1)}, bf16[384,1024]{1,0:T(8,128)(2,1)S(1)}, u32[]{:S(2)}, u32[]{:S(2)}) collective-permute-start(bf16[384,1024]{1,0:T(8,128)(2,1)S(1)} %collective-permute-done.2.refs_1_), channel_id=1, source_target_pairs={{0,1},{1,2},{2,3},{3,0},{4,5},{5,6},{6,7},{7,4},{8,9},{9,10},{10,1... | collective-permute-start | bytes 2359304 | tf_op jit(solution)/shard_map/ppermute | solution.py:300
  68.8 37.5 %collective-permute-start.7 = (bf16[384,768]{1,0:T(8,128)(2,1)S(1)}, bf16[384,768]{1,0:T(8,128)(2,1)S(1)}, u32[]{:S(2)}, u32[]{:S(2)}) collective-permute-start(bf16[384,768]{1,0:T(8,128)(2,1)S(1)} %collective-permute-done.1.refs_1_), channel_id=1, source_target_pairs={{0,1},{1,2},{2,3},{3,0},{4,5},{5,6},{6,7},{7,4},{8,9},{9,10},{10,1... | collective-permute-start | bytes 1769480 | tf_op jit(solution)/shard_map/ppermute | solution.py:300
  68.9 51.9 %collective-permute-start.6 = (bf16[384,1024]{1,0:T(8,128)(2,1)S(1)}, bf16[384,1024]{1,0:T(8,128)(2,1)S(1)}, u32[]{:S(2)}, u32[]{:S(2)}) collective-permute-start(bf16[384,1024]{1,0:T(8,128)(2,1)S(1)} %collective-permute-done.refs_1_), channel_id=1, source_target_pairs={{0,1},{1,2},{2,3},{3,0},{4,5},{5,6},{6,7},{7,4},{8,9},{9,10},{10,1... | collective-permute-start | bytes 2359304 | tf_op jit(solution)/shard_map/ppermute | solution.py:300
  106.4 64.1 %collective-permute-start.16 = (bf16[384,1024]{1,0:T(8,128)(2,1)S(1)}, bf16[384,1024]{1,0:T(8,128)(2,1)S(1)}, u32[]{:S(2)}, u32[]{:S(2)}) collective-permute-start(bf16[384,1024]{1,0:T(8,128)(2,1)S(1)} %collective-permute-done.8.refs_2_), channel_id=1, source_target_pairs={{0,1},{1,2},{2,3},{3,0},{4,5},{5,6},{6,7},{7,4},{8,9},{9,10},{10,1... | collective-permute-start | bytes 2359304 | tf_op jit(solution)/shard_map/ppermute | solution.py:300
  108.4 62.1 %collective-permute-start.15 = (bf16[384,768]{1,0:T(8,128)(2,1)S(1)}, bf16[384,768]{1,0:T(8,128)(2,1)S(1)}, u32[]{:S(2)}, u32[]{:S(2)}) collective-permute-start(bf16[384,768]{1,0:T(8,128)(2,1)S(1)} %collective-permute-done.7.refs_2_), channel_id=1, source_target_pairs={{0,1},{1,2},{2,3},{3,0},{4,5},{5,6},{6,7},{7,4},{8,9},{9,10},{10,1... | collective-permute-start | bytes 1769480 | tf_op jit(solution)/shard_map/ppermute | solution.py:300
  109.0 39.3 %collective-permute-start.12 = (f32[1,3840]{1,0:T(1,128)}, f32[1,3840]{1,0:T(1,128)S(1)}, u32[]{:S(2)}, u32[]{:S(2)}) collective-permute-start(f32[1,3840]{1,0:T(1,128)} %shard_map.147.refs_0_), channel_id=1, source_target_pairs={{0,1},{1,0},{2,3},{3,2},{4,5},{5,4},{6,7},{7,6},{8,9},{9,8},{10,11... | collective-permute-start | bytes 46088 | tf_op jit(solution)/shard_map/ppermute | solution.py:27
  109.3 39.3 %collective-permute-start.13 = (f32[1,3840]{1,0:T(1,128)}, f32[1,3840]{1,0:T(1,128)S(1)}, u32[]{:S(2)}, u32[]{:S(2)}) collective-permute-start(f32[1,3840]{1,0:T(1,128)} %shard_map.147.refs_0_), channel_id=1, source_target_pairs={{0,2},{1,3},{2,0},{3,1},{4,6},{5,7},{6,4},{7,5},{8,10},{9,11},{10,... | collective-permute-start | bytes 46088 | tf_op jit(solution)/shard_map/ppermute | solution.py:27
  120.8 27.8 %collective-permute-start.14 = (f32[1,3840]{1,0:T(1,128)}, f32[1,3840]{1,0:T(1,128)S(1)}, u32[]{:S(2)}, u32[]{:S(2)}) collective-permute-start(f32[1,3840]{1,0:T(1,128)} %shard_map.147.refs_0_), channel_id=1, source_target_pairs={{0,3},{1,2},{2,1},{3,0},{4,7},{5,6},{6,5},{7,4},{8,11},{9,10},{10,... | collective-permute-start | bytes 46088 | tf_op jit(solution)/shard_map/ppermute | solution.py:27
  148.6 35.1 %collective-permute-start.24 = (bf16[384,1024]{1,0:T(8,128)(2,1)S(1)}, bf16[384,1024]{1,0:T(8,128)(2,1)S(1)}, u32[]{:S(2)}, u32[]{:S(2)}) collective-permute-start(bf16[384,1024]{1,0:T(8,128)(2,1)S(1)} %collective-permute-done.6.refs_2_), channel_id=1, source_target_pairs={{0,1},{1,2},{2,3},{3,0},{4,5},{5,6},{6,7},{7,4},{8,9},{9,10},{10,1... | collective-permute-start | bytes 2359304 | tf_op jit(solution)/shard_map/ppermute | solution.py:300
  170.5 14.0 %collective-permute-start.25 = (bf16[384,512]{1,0:T(8,128)(2,1)S(1)}, bf16[384,512]{1,0:T(8,128)(2,1)}, u32[]{:S(2)}, u32[]{:S(2)}) collective-permute-start(bf16[384,512]{1,0:T(8,128)(2,1)S(1)} %get-tuple-element.102.refs_0_), channel_id=1, source_target_pairs={{0,1},{1,2},{2,3},{3,0},{4,5},{5,6},{6,7},{7,4},{8,9},{9,10},{10,1... | collective-permute-start | bytes 1179656 | tf_op jit(solution)/shard_map/ppermute | solution.py:300
  171.3 26.6 %collective-permute-start.23 = (bf16[384,512]{1,0:T(8,128)(2,1)S(1)}, bf16[384,512]{1,0:T(8,128)(2,1)S(1)}, u32[]{:S(2)}, u32[]{:S(2)}) collective-permute-start(bf16[384,512]{1,0:T(8,128)(2,1)S(1)} %get-tuple-element.96.refs_0_), channel_id=1, source_target_pairs={{0,1},{1,2},{2,3},{3,0},{4,5},{5,6},{6,7},{7,4},{8,9},{9,10},{10,1... | collective-permute-start | bytes 1179656 | tf_op jit(solution)/shard_map/ppermute | solution.py:300
  184.5 21.6 %collective-permute-start.27 = (bf16[384,512]{1,0:T(8,128)(2,1)}, bf16[384,512]{1,0:T(8,128)(2,1)S(1)}, u32[]{:S(2)}, u32[]{:S(2)}) collective-permute-start(bf16[384,512]{1,0:T(8,128)(2,1)} %collective-permute-done.25.refs_1_), channel_id=1, source_target_pairs={{0,1},{1,2},{2,3},{3,0},{4,5},{5,6},{6,7},{7,4},{8,9},{9,10},{10,1... | collective-permute-start | bytes 1179656 | tf_op jit(solution)/shard_map/ppermute | solution.py:300
  197.9 10.0 %collective-permute-start.26 = (bf16[384,512]{1,0:T(8,128)(2,1)S(1)}, bf16[384,512]{1,0:T(8,128)(2,1)S(1)}, u32[]{:S(2)}, u32[]{:S(2)}) collective-permute-start(bf16[384,512]{1,0:T(8,128)(2,1)S(1)} %collective-permute-done.23.refs_1_), channel_id=1, source_target_pairs={{0,1},{1,2},{2,3},{3,0},{4,5},{5,6},{6,7},{7,4},{8,9},{9,10},{10,1... | collective-permute-start | bytes 1179656 | tf_op jit(solution)/shard_map/ppermute | solution.py:300
  200.3 11.2 %collective-permute-start.20 = (f32[2,128]{1,0:T(2,128)}, f32[2,128]{1,0:T(2,128)S(1)}, u32[]{:S(2)}, u32[]{:S(2)}) collective-permute-start(f32[2,128]{1,0:T(2,128)} %get-tuple-element.95.refs_2_), channel_id=1, source_target_pairs={{0,1},{1,0},{2,3},{3,2},{4,5},{5,4},{6,7},{7,6},{8,9},{9,8},{10,11... | collective-permute-start | bytes 3080 | tf_op jit(solution)/shard_map/ppermute | solution.py:27
  201.0 10.4 %collective-permute-start.21 = (f32[2,128]{1,0:T(2,128)}, f32[2,128]{1,0:T(2,128)S(1)}, u32[]{:S(2)}, u32[]{:S(2)}) collective-permute-start(f32[2,128]{1,0:T(2,128)} %get-tuple-element.95.refs_2_), channel_id=1, source_target_pairs={{0,2},{1,3},{2,0},{3,1},{4,6},{5,7},{6,4},{7,5},{8,10},{9,11},{10,... | collective-permute-start | bytes 3080 | tf_op jit(solution)/shard_map/ppermute | solution.py:27
  207.9 28.8 %collective-permute-start.29 = (bf16[384,512]{1,0:T(8,128)(2,1)S(1)}, bf16[384,512]{1,0:T(8,128)(2,1)S(1)}, u32[]{:S(2)}, u32[]{:S(2)}) collective-permute-start(bf16[384,512]{1,0:T(8,128)(2,1)S(1)} %collective-permute-done.27.refs_2_), channel_id=1, source_target_pairs={{0,1},{1,2},{2,3},{3,0},{4,5},{5,6},{6,7},{7,4},{8,9},{9,10},{10,1... | collective-permute-start | bytes 1179656 | tf_op jit(solution)/shard_map/ppermute | solution.py:300
  207.9 37.2 %collective-permute-start.28 = (bf16[384,512]{1,0:T(8,128)(2,1)S(1)}, bf16[384,512]{1,0:T(8,128)(2,1)S(1)}, u32[]{:S(2)}, u32[]{:S(2)}) collective-permute-start(bf16[384,512]{1,0:T(8,128)(2,1)S(1)} %collective-permute-done.26.refs_2_), channel_id=1, source_target_pairs={{0,1},{1,2},{2,3},{3,0},{4,5},{5,6},{6,7},{7,4},{8,9},{9,10},{10,1... | collective-permute-start | bytes 1179656 | tf_op jit(solution)/shard_map/ppermute | solution.py:300
  (50 other events, 673.3 us)
Sparse Core Ops, SparseCore 0:
  9.9 41.6 all-gather.2
  53.4 99.3 all-gather.4

commit v2 on v1

--- a/solution.py
+++ b/solution.py
@@ -9,7 +9,7 @@
 
 EPS = 1e-06
 LANES = 128
-PARAMS = pltpu.CompilerParams(vmem_limit_bytes=56 * 1024 * 1024)
+PARAMS = pltpu.CompilerParams(vmem_limit_bytes=28 * 1024 * 1024)
 F32 = jnp.float32
 BF16 = jnp.bfloat16
 
@@ -162,11 +162,16 @@
     )(total)
 
 
-def grad_chunk(order, blocks, inputs, weight, chunk, buffer, inner, which):
-    count = len(blocks)
-    tokens, width = blocks[0].shape
-    depth, columns = inputs.shape
+def grad_chunk(order, blocks, inputs, weight, row, columns, buffer, inner, which):
+    flat = [array for arrays in blocks for array in arrays]
+    count = len(flat)
+    tokens = flat[0].shape[0]
+    width = sum(array.shape[1] for array in blocks[0])
+    depth = inputs.shape[0]
+    first, columns = columns
     tile = tile_of(columns, 512)
+    chunk, first = row // width, first // tile
+    resident = pl.BlockSpec(memory_space=pltpu.VMEM)
 
     def kernel(order_ref, *refs):
         x_ref, w_ref, before_ref = refs[count : count + 3]
@@ -175,27 +180,33 @@
         @pl.when(pl.program_id(0) == 0)
         def _():
             inner_ref[...] = before_ref[...]
-            for slot in range(count):
+            position = 0
+            for slot, arrays in enumerate(blocks):
                 start = pl.multiple_of(order_ref[slot] * tokens, LANES)
-                turned[:, pl.ds(start, tokens)] = refs[slot][...].T
+                top = 0
+                for array in arrays:
+                    turned[top : top + array.shape[1], pl.ds(start, tokens)] = refs[position][...].T
+                    top += array.shape[1]
+                    position += 1
 
         here = slice(8 * which, 8 * which + 8)
         total = jnp.dot(turned[...], x_ref[...], preferred_element_type=F32)
-        g_ref[...] = total.astype(g_ref.dtype)
+        start = pl.multiple_of((first + pl.program_id(0)) * tile, LANES)
+        g_ref[row : row + width, pl.ds(start, tile)] = total.astype(g_ref.dtype)
         product = total * w_ref[...].astype(F32)
         product = jnp.sum(product.reshape(-1, 8, tile), axis=0)
         inner_ref[here, :] += sum(product[:, c : c + LANES] for c in range(0, tile, LANES))
 
-    in_specs = [pl.BlockSpec((tokens, width), lambda j, o: (0, 0)) for _ in blocks]
+    in_specs = [pl.BlockSpec(array.shape, lambda j, o: (0, 0)) for array in flat]
     in_specs += [
-        pl.BlockSpec((depth, tile), lambda j, o: (0, j)),
-        pl.BlockSpec((width, tile), lambda j, o: (chunk, j)),
-        pl.BlockSpec((16, LANES), lambda j, o: (0, 0)),
+        pl.BlockSpec((depth, tile), lambda j, o: (0, first + j)),
+        pl.BlockSpec((width, tile), lambda j, o: (chunk, first + j)),
+        whole(inner),
     ]
-    operands = [order, *blocks, inputs, weight, inner]
+    operands = [order, *flat, inputs, weight, inner]
     aliases = {}
     if buffer is not None:
-        in_specs.append(pl.BlockSpec(memory_space=pl.ANY))
+        in_specs.append(resident)
         operands.append(buffer)
         aliases = {count + 4: 0}
     return pl.pallas_call(
@@ -205,62 +216,73 @@
             grid=(columns // tile,),
             in_specs=in_specs,
             out_specs=[
-                pl.BlockSpec((width, tile), lambda j, o: (chunk, j)),
-                pl.BlockSpec((16, LANES), lambda j, o: (0, 0)),
+                resident,
+                whole(inner),
             ],
             scratch_shapes=[pltpu.VMEM((width, depth), BF16)],
         ),
         out_shape=[
-            jax.ShapeDtypeStruct(weight.shape, BF16),
-            jax.ShapeDtypeStruct((16, LANES), F32),
+            pltpu.VMEM(weight.shape, BF16),
+            jax.ShapeDtypeStruct(inner.shape, F32),
         ],
         input_output_aliases=aliases,
-        compiler_params=PARAMS,
+        compiler_params=pltpu.CompilerParams(vmem_limit_bytes=36 * 1024 * 1024),
+        cost_estimate=pl.CostEstimate(
+            flops=2 * depth * width * columns,
+            bytes_accessed=2 * (depth * width + depth * columns + 2 * width * columns),
+            transcendentals=0,
+        ),
     )(*operands)
 
 
-def finish(grads, left, norms, rights, squares, inners, gains):
+def finish(grads, left, norms, rights, terms, factors):
     heights, steps = row_blocks(grads)
     extents = [g.shape[0] for g in grads]
     spans = [g.shape[1] for g in grads]
-    count = len(squares)
-
-    def kernel(left_ref, norms_ref, *refs):
-        v_refs, refs = refs[:2], refs[2:]
-        square_refs, refs = refs[:count], refs[count:]
-        inner_refs, refs = refs[:count], refs[count:]
-        gains_ref, refs = refs[0], refs[1:]
-        g_refs, out_refs, gain_ref = refs[:2], refs[2:4], refs[4]
+    count = len(terms)
+
+    def kernel(factors_ref, left_ref, norms_ref, *refs):
+        right_refs, refs = refs[:2], refs[2:]
+        term_refs, refs = refs[:count], refs[count:]
+        g_refs, out_refs, gain_ref, v_refs = refs[:2], refs[2:4], refs[4], refs[5:]
         step = pl.program_id(0)
-        square = tree([ref[...] for ref in square_refs])
-        inner = tree([ref[...] for ref in inner_refs])
+
+        @pl.when(step == 0)
+        def _():
+            total = tree([ref[...] for ref in term_refs])
+            for k in range(2):
+                gain, sigma = factors_ref[0, k], factors_ref[1, k]
+                gw = jnp.sum(total[8 * k : 8 * k + 8])
+                gain_ref[k] = gw / sigma
+                v_refs[k][...] = gain * gw / (sigma * sigma) * right_refs[k][...]
+
         row = 0
         for k in range(2):
-            sigma = norm_of(square[k : k + 1])
-            gw = jnp.sum(jnp.sum(inner[8 * k : 8 * k + 8], axis=0, keepdims=True), axis=1, keepdims=True)
-            gain = gains_ref[k : k + 1, :1]
-            scale = gain / sigma
-            slope = gain * gw / (sigma * sigma)
-            gain_ref[k : k + 1, :] = jnp.broadcast_to(gw / sigma, (1, LANES))
+            scale = factors_ref[0, k] / factors_ref[1, k]
+            top = pl.multiple_of(step * heights[k], LANES)
             start = pl.multiple_of(row + step * heights[k], LANES)
             norm = norm_of(norms_ref[:, k * LANES : (k + 1) * LANES])
             column = column_of((left_ref[:, pl.ds(start, heights[k])] / norm).astype(BF16).astype(F32))
-            for c in range(0, spans[k], LANES):
-                here = slice(c, c + LANES)
-                v = slope * (v_refs[k][:, here] / sigma)
-                out_refs[k][:, here] = (scale * g_refs[k][:, here].astype(F32) - column * v).astype(BF16)
+            for r in range(0, heights[k], 64):
+                part = column[r : r + 64]
+                for c in range(0, spans[k], LANES):
+                    here = slice(c, c + LANES)
+                    g = g_refs[k][pl.ds(top + r, 64), here].astype(F32)
+                    out_refs[k][r : r + 64, here] = (scale * g - part * v_refs[k][:, here]).astype(BF16)
             row += extents[k]
 
-    operands = [left, norms, *rights, *squares, *inners, gains]
+    operands = [left, norms, *rights, *terms]
     blocks = [pl.BlockSpec((heights[k], spans[k]), lambda i: (i, 0)) for k in range(2)]
+    smem = pl.BlockSpec(memory_space=pltpu.SMEM)
     return pl.pallas_call(
         kernel,
         grid=(steps,),
-        in_specs=[whole(o) for o in operands] + blocks,
-        out_specs=blocks + [pl.BlockSpec((2, LANES), lambda i: (0, 0))],
-        out_shape=[jax.ShapeDtypeStruct(g.shape, BF16) for g in grads] + [jax.ShapeDtypeStruct((2, LANES), F32)],
-        compiler_params=PARAMS,
-    )(*operands, *grads)
+        in_specs=[smem] + [whole(o) for o in operands] + [pl.BlockSpec(memory_space=pltpu.VMEM)] * 2,
+        out_specs=blocks + [smem],
+        out_shape=[jax.ShapeDtypeStruct(g.shape, BF16) for g in grads] + [jax.ShapeDtypeStruct((2,), F32)],
+        scratch_shapes=[pltpu.VMEM((1, span), F32) for span in spans],
+        compiler_params=pltpu.CompilerParams(vmem_limit_bytes=36 * 1024 * 1024),
+    )(factors, *operands, *grads)
 
 
 def local(
@@ -277,90 +299,81 @@
     vector_down,
 ):
     weights = (weight_up, weight_down)
-    inputs_all = (
-        lax.all_gather(inputs_up, "row", axis=0, tiled=True),
-        lax.all_gather(inputs_down, "row", axis=0, tiled=True),
-    )
+    inputs = [lax.all_gather(array, "row", axis=0, tiled=True) for array in (inputs_up, inputs_down)]
     extents = (weight_up.shape[0], weight_down.shape[0])
     spans = (weight_up.shape[1], weight_down.shape[1])
     ring = [(i, (i + 1) % cols) for i in range(cols)]
     order = lax.rem(lax.axis_index("col") - jnp.arange(cols, dtype=jnp.int32) + cols, jnp.int32(cols))
-    gains = jnp.broadcast_to(gain_pair[:, None], (2, LANES))
-
-    unit = grads_up.shape[1] // 6
-    chunks = [
-        [grads_down, grads_up[:, : 2 * unit]],
-        [grads_up[:, 2 * unit : 4 * unit]],
-        [grads_up[:, 4 * unit : 5 * unit]],
-        [grads_up[:, 5 * unit :]],
-    ]
-    streams = [[chunk] for chunk in chunks]
-
-    def hop(pieces):
-        return [lax.ppermute(piece, "col", ring) for piece in pieces]
-
-    def advance(number, *others):
-        held, *others = fence(streams[number][-1], *others)
-        streams[number][-1] = held
-        streams[number].append(hop(held))
-        return others
-
-    def land(number, *others):
-        held, *others = fence(streams[number][-1], *others)
-        streams[number][-1] = held
-        return others
-
-    grad_ws = [None, None]
-    inner = jnp.zeros((16, LANES), F32)
-
-    def multiply(k, number, place, chunk):
-        slots = [pieces[place] for pieces in streams[number]]
-        return grad_chunk(order, slots, inputs_all[k], weights[k], chunk, grad_ws[k], inner, k)
-
-    streams[0].append(hop(chunks[0]))
-    streams[1].append(hop(chunks[1]))
+
+    third = grads_up.shape[1] // 3
+    held = {name: [grads_up[:, c * third : (c + 1) * third]] for c, name in enumerate("uvc")}
+    held["d"] = [grads_down]
+
+    def send(*names):
+        for name in names:
+            held[name].append(lax.ppermute(held[name][-1], "col", ring))
+
+    def when(names, *values):
+        got, *values = fence([held[name][-1] for name in names], *values)
+        for name, block in zip(names, got):
+            held[name][-1] = block
+        return values if len(values) > 1 else values[0]
+
+    grads = [None, None]
+
+    def multiply(k, names, row, inner, part=0, parts=1):
+        blocks = list(zip(*(held[name] for name in names)))
+        columns = (part * spans[k] // parts, spans[k] // parts)
+        grads[k], inner = grad_chunk(order, blocks, inputs[k], weights[k], row, columns, grads[k], inner, k)
+        return inner
+
+    send("d", "u")
     part = left_product((vector_up[None, :], vector_down[None, :]), weights)
     terms = exchange(part, "col", cols)
-    (terms,) = advance(0, terms)
-    (terms,) = advance(1, terms)
+    terms = when("du", terms)
+    send("d", "u")
     left, total = right_product(terms, weights)
-    *rights, _ = scale_right(all_sum(total, "row", rows), spans)
+    total = when("d", all_sum(total, "row", rows))
+    send("d")
+    *rights, _ = scale_right(total, spans)
     part = left_product(rights, weights)
-    (part,) = advance(0, part)
     terms = exchange(part, "col", cols)
-    (terms,) = advance(1, terms)
+    terms = when("udvc", terms)
+    send("u", "v", "c")
     left, total = right_product(terms, weights)
-    total = all_sum(total, "row", rows)
-    for _ in range(cols - 4):
-        (total,) = advance(0, total)
-        (total,) = advance(1, total)
-    (total,) = land(0, total)
-    (total,) = advance(2, total)
+    total = when("u", all_sum(total, "row", rows))
     *rights, square = scale_right(total, spans)
     squares = exchange(square, "col", cols)
-    (inner,) = advance(3, inner)
-    grad_ws[0], inner = multiply(0, 0, 1, 0)
-    (inner,) = land(1, inner)
-    for step in range(cols - 2):
-        (inner,) = advance(2, inner)
-        if step == 0:
-            grad_ws[0], inner = multiply(0, 1, 0, 1)
-        (inner,) = advance(3, inner)
-    grad_ws[1], inner = multiply(1, 0, 0, 0)
-    (inner,) = land(2, inner)
-    grad_ws[0], inner = multiply(0, 2, 0, 4)
-    (inner,) = land(3, inner)
-    grad_ws[0], inner = multiply(0, 3, 0, 5)
-    inners = exchange(all_sum(inner, "row", rows), "col", cols)
+    inner = jnp.zeros((16, LANES), F32)
+    for _ in range(cols - 4):
+        inner = when("udvc", inner)
+        send("u", "d", "v", "c")
+    inner = when("v", inner)
+    send("v")
+    inner = multiply(0, "u", 0, inner)
+    inner, squares = when("c", inner, squares)
+    send("c")
     norms = total[:, sum(spans) :]
-    wgrad_up, wgrad_down, gain_grads = finish(grad_ws, left, norms, rights, squares, inners, gains)
-
     norm = jnp.sqrt(jnp.sum(norms.reshape(2, LANES), axis=1) + EPS)
     sigma = jnp.sqrt(jnp.sum(tree(squares), axis=1) + EPS)
-    left_up = left[0, : extents[0]] / norm[0]
-    left_down = left[0, extents[0] :] / norm[1]
-    right_up, right_down = (rights[k][0] / sigma[k] for k in range(2))
-    return wgrad_up, wgrad_down, gain_grads[:, 0], left_up, right_up, left_down, right_down
+    vectors = [left[0, : extents[0]] / norm[0], left[0, extents[0] :] / norm[1]]
+    rights = [rights[k] / sigma[k] for k in range(2)]
+    vectors += [row[0] for row in rights]
+    inner = multiply(1, "d", 0, inner, 0, 2)
+    inner, vectors, rights, sigma = when("v", inner, vectors, rights, sigma)
+    send("v")
+    inner = multiply(1, "d", 0, inner, 1, 2)
+    inner = when("c", inner)
+    send("c")
+    inner = when("v", inner)
+    inner = multiply(0, "v", third, inner)
+    inner = when("c", inner)
+    inner = multiply(0, "c", 2 * third, inner)
+    terms = exchange(all_sum(inner, "row", rows), "col", cols)
+    factors = jnp.stack([gain_pair, sigma])
+    wgrad_up, wgrad_down, gain_grads = finish(grads, left, norms, rights, terms, factors)
+    left_up, left_down, right_up, right_down = vectors
+    return wgrad_up, wgrad_down, gain_grads, left_up, right_up, left_down, right_down
 
 
 def solution(mesh):

time: 297 us -> 261 us (0.88)
  Pallas kernels: 122 us -> 81.5 us
  local copies, waits for them, and re-layouts: 10.3 us -> 42 us
  waiting for transfers between devices: 95.4 us -> 76.4 us
  other arithmetic: 10.1 us -> 4.94 us
  starting transfers between devices: 44 us -> 40.7 us
    unnamed x72 -> x60, local copies, waits for them, and re-layouts: 2 us -> 38.3 us
    ppermute x12, waiting for transfers between devices: 66.8 us -> 31.4 us  [exchange(): lax.ppermute(value, axis, [(i, i ^ k) for i in range(size)])]
    ppermute x15 -> x12, waiting for transfers between devices: 10.6 us -> 26.3 us  [send(): held[name].append(lax.ppermute(held[name][-1], 'col', ring))]
    pallas_call x2, Pallas kernels: 21.7 us -> 8.7 us  [left_product(): pl.pallas_call(kernel, grid=(steps,), in_specs=[whole(r) for r in rights]...]
    pallas_call x5, Pallas kernels: 61.8 us -> 50.1 us  [grad_chunk(): pl.pallas_call(kernel, grid_spec=pltpu.PrefetchScalarGridSpec(num_scalar_...]
    pallas_call x2, Pallas kernels: 20.1 us -> 9.52 us  [right_product(): pl.pallas_call(kernel, grid=(steps,), in_specs=[whole(t) for t in terms]...]
    ppermute x15 -> x12, starting transfers between devices: 17.7 us -> 13.4 us  [send(): held[name].append(lax.ppermute(held[name][-1], 'col', ring))]
    add x9, other arithmetic: 3.64 us -> 0.21 us  [all_sum(): value + lax.ppermute(value, axis, [(i, i ^ step) for i in range(size)])]
  transfers between devices with their start and end apart: 38 -> 35, of which waited for: 17 -> 20; matrix products, arithmetic and copies ran while one was open for 5% -> 3% of each run, Pallas kernels for 33% -> 23%
where the time goes in v2:
time: 261 us; the launch traced here: 260 us
  Pallas kernels  81.5 us (31%)
  waiting for transfers between devices  76.4 us (29%)
  local copies, waits for them, and re-layouts  42 us (16%)
  starting transfers between devices  40.7 us (16%)
  between operations  14.4 us (6%)
  other arithmetic  4.94 us (2%)
    pallas_call x5, Pallas kernels, grad_chunk(): pl.pallas_call(kernel, grid_spec=pltpu.PrefetchScalarGridSpec(num_scalar_...  50.1 us
    unnamed x60, local copies, waits for them, and re-layouts  38.3 us
    ppermute x12, waiting for transfers between devices, exchange(): lax.ppermute(value, axis, [(i, i ^ k) for i in range(size)])  31.4 us
    ppermute x12, waiting for transfers between devices, send(): held[name].append(lax.ppermute(held[name][-1], 'col', ring))  26.3 us
    ppermute x12, starting transfers between devices, exchange(): lax.ppermute(value, axis, [(i, i ^ k) for i in range(size)])  17.7 us
    ppermute x9, waiting for transfers between devices, all_sum(): lax.ppermute(value, axis, [(i, i ^ step) for i in range(size)])  17.3 us
    ppermute x12, starting transfers between devices, send(): held[name].append(lax.ppermute(held[name][-1], 'col', ring))  13.4 us
    pallas_call x1, Pallas kernels, finish(): pl.pallas_call(kernel, grid=(steps,), in_specs=[smem] + [whole(o) for o i...  12.3 us
  transfers between devices with their start and end apart: 35, of which 20 were waited for; matrix products, arithmetic and copies ran while one was open for 3% of the time, Pallas kernels for 23%

profile of v2, /device:TPU:0, one launch (start us, length us, event | category | flops | bytes accessed | tf_op | source)
XLA Modules:
  0.0 259.9 jit_solution(1006835509878646791)
XLA Ops:
  15.8 3.8 %copy-done = bf16[768,6144]{1,0:T(8,128)(2,1)S(1)} copy-done((bf16[768,6144]{1,0:T(8,128)(2,1)S(1)}, bf16[768,6144]{1,0:T(8,128)(2,1)}, u32[]{:S(2)}) %copy-start) | copy-done | bytes 9437208
  19.6 3.9 %copy-done.1 = bf16[3072,1536]{1,0:T(8,128)(2,1)S(1)} copy-done((bf16[3072,1536]{1,0:T(8,128)(2,1)S(1)}, bf16[3072,1536]{1,0:T(8,128)(2,1)}, u32[]{:S(2)}) %copy-start.1) | copy-done | bytes 9437208
  24.3 4.4 %shard_map.144.refs_0_ = f32[1,3840]{1,0:T(1,128)S(1)} custom-call(f32[1,1536]{1,0:T(1,128)S(1)} %broadcast_in_dim.9.v_up_ref, f32[1,6144]{1,0:T(1,128)S(1)} %bitcast.15, bf16[3072,1536]{1,0:T(8,128)(2,1)S(1)} %copy-done.1, bf16[768,6144]{1,0:T(8,128)(2,1)S(1)} %copy-done), custom_call_target="tpu_custom_call" | custom-call | tf_op jit(solution)/shard_map/pallas_call | solution.py:89
  33.2 13.4 %collective-permute-done.2.refs_1_ = f32[1,3840]{1,0:T(1,128)S(1)} collective-permute-done((f32[1,3840]{1,0:T(1,128)S(1)}, f32[1,3840]{1,0:T(1,128)S(1)}, u32[]{:S(2)}, u32[]{:S(2)}) %collective-permute-start.2) | collective-permute-done | bytes 15392 | tf_op jit(solution)/shard_map/ppermute | solution.py:27
  48.5 5.0 %shard_map.145 = (f32[1,3840]{1,0:T(1,128)}, f32[1,7936]{1,0:T(1,128)S(1)}) custom-call(f32[1,3840]{1,0:T(1,128)S(1)} %shard_map.144.refs_0_, f32[1,3840]{1,0:T(1,128)S(1)} %collective-permute-done.2.refs_1_, f32[1,3840]{1,0:T(1,128)S(1)} %collective-permute-done.3.refs_2_, f32[1,3840]{1,0:T(1,128)S(1)} %collective-permute-done.4.refs_3_, ...), custom_call_target="tpu_custom_call" | custom-call | tf_op jit(solution)/shard_map/pallas_call | solution.py:134
  65.8 3.7 %copy-done.2 = bf16[3072,1536]{1,0:T(8,128)(2,1)S(1)} copy-done((bf16[3072,1536]{1,0:T(8,128)(2,1)S(1)}, bf16[3072,1536]{1,0:T(8,128)(2,1)}, u32[]{:S(2)}) %copy-start.2) | copy-done | bytes 9437208
  69.5 4.4 %shard_map.147.refs_0_ = f32[1,3840]{1,0:T(1,128)S(1)} custom-call(f32[1,1536]{1,0:T(1,128)S(1)} %get-tuple-element.78.v_up_ref, f32[1,6144]{1,0:T(1,128)S(1)} %get-tuple-element.79.v_down_ref, bf16[3072,1536]{1,0:T(8,128)(2,1)S(1)} %copy-done.2, bf16[768,6144]{1,0:T(8,128)(2,1)S(1)} %bitcast.11), custom_call_target="tpu_custom_call" | custom-call | tf_op jit(solution)/shard_map/pallas_call | solution.py:89
  78.3 15.6 %collective-permute-done.11.refs_1_ = f32[1,3840]{1,0:T(1,128)S(1)} collective-permute-done((f32[1,3840]{1,0:T(1,128)S(1)}, f32[1,3840]{1,0:T(1,128)S(1)}, u32[]{:S(2)}, u32[]{:S(2)}) %collective-permute-start.11) | collective-permute-done | bytes 15392 | tf_op jit(solution)/shard_map/ppermute | solution.py:27
  95.9 4.5 %shard_map.148 = (f32[1,3840]{1,0:T(1,128)S(1)}, f32[1,7936]{1,0:T(1,128)S(1)}) custom-call(f32[1,3840]{1,0:T(1,128)S(1)} %shard_map.147.refs_0_, f32[1,3840]{1,0:T(1,128)S(1)} %collective-permute-done.11.refs_1_, f32[1,3840]{1,0:T(1,128)S(1)} %collective-permute-done.12.refs_2_, f32[1,3840]{1,0:T(1,128)S(1)} %collective-permute-done.13.refs_3_, ...), custom_call_target="tpu_custom_call" | custom-call | tf_op jit(solution)/shard_map/pallas_call | solution.py:134
  111.1 6.5 %collective-permute-done.17.refs_3_ = bf16[384,1024]{1,0:T(8,128)(2,1)} collective-permute-done((bf16[384,1024]{1,0:T(8,128)(2,1)}, bf16[384,1024]{1,0:T(8,128)(2,1)}, u32[]{:S(2)}, u32[]{:S(2)}) %collective-permute-start.17) | collective-permute-done | bytes 786464 | tf_op jit(solution)/shard_map/ppermute | solution.py:314
  118.0 4.3 %collective-permute-start.23 = (f32[2,128]{1,0:T(2,128)S(1)}, f32[2,128]{1,0:T(2,128)S(1)}, u32[]{:S(2)}, u32[]{:S(2)}) collective-permute-start(f32[2,128]{1,0:T(2,128)S(1)} %get-tuple-element.99), channel_id=1, source_target_pairs={{0,3},{1,2},{2,1},{3,0},{4,7},{5,6},{6,5},{7,4},{8,11},{9,10},{10,... | collective-permute-start | bytes 3080 | tf_op jit(solution)/shard_map/ppermute | solution.py:27
  122.3 12.3 %collective-permute-done.14.refs_1_ = bf16[384,1024]{1,0:T(8,128)(2,1)} collective-permute-done((bf16[384,1024]{1,0:T(8,128)(2,1)S(1)}, bf16[384,1024]{1,0:T(8,128)(2,1)}, u32[]{:S(2)}, u32[]{:S(2)}) %collective-permute-start.14) | collective-permute-done | bytes 786464 | tf_op jit(solution)/shard_map/ppermute | solution.py:314
  142.7 8.8 %shard_map.149 = (bf16[3072,1536]{1,0:T(8,128)(2,1)S(1)}, f32[16,128]{1,0:T(8,128)S(1)}) custom-call(s32[4]{0:T(128)S(1)} %compare_select_fusion.order_ref, bf16[384,1024]{1,0:T(8,128)(2,1)S(1)} %copy-done.18, bf16[384,1024]{1,0:T(8,128)(2,1)S(1)} %copy-done.22, bf16[384,1024]{1,0:T(8,128)(2,1)} %collective-permute-done.5.refs_2_, ...), custom_call_target="tpu_custom_call" | custom-call | flops 4831838208 | bytes 14155776 | tf_op jit(solution)/shard_map/pallas_call | solution.py:212
  151.5 3.7 %copy-done.3 = bf16[3072,1536]{1,0:T(8,128)(2,1)} copy-done((bf16[3072,1536]{1,0:T(8,128)(2,1)}, bf16[3072,1536]{1,0:T(8,128)(2,1)S(1)}, u32[]{:S(2)}) %copy-start.3) | copy-done | bytes 9437208
  161.2 12.0 %shard_map.151 = (bf16[768,6144]{1,0:T(8,128)(2,1)S(1)}, f32[16,128]{1,0:T(8,128)S(1)}) custom-call(s32[4]{0:T(128)S(1)} %compare_select_fusion.order_ref, bf16[384,768]{1,0:T(8,128)(2,1)S(1)} %copy-done.9, bf16[384,768]{1,0:T(8,128)(2,1)S(1)} %copy-done.11, bf16[384,768]{1,0:T(8,128)(2,1)S(1)} %copy-done.14, bf16[384,768]{1,0:T(8,128)(2,1)S(1)} %copy-done.16, ...), custom_call_target="tpu_custom_call" | custom-call | flops 7247757312 | bytes 21233664 | tf_op jit(solution)/shard_map/pallas_call | solution.py:212
  173.3 3.7 %copy-done.4 = bf16[768,6144]{1,0:T(8,128)(2,1)} copy-done((bf16[768,6144]{1,0:T(8,128)(2,1)}, bf16[768,6144]{1,0:T(8,128)(2,1)S(1)}, u32[]{:S(2)}) %copy-start.4) | copy-done | bytes 9437208
  177.2 3.7 %copy-done.5 = bf16[768,6144]{1,0:T(8,128)(2,1)S(1)} copy-done((bf16[768,6144]{1,0:T(8,128)(2,1)S(1)}, bf16[768,6144]{1,0:T(8,128)(2,1)}, u32[]{:S(2)}) %copy-start.5) | copy-done | bytes 9437208
  180.9 11.8 %shard_map.152 = (bf16[768,6144]{1,0:T(8,128)(2,1)S(1)}, f32[16,128]{1,0:T(8,128)S(1)}) custom-call(s32[4]{0:T(128)S(1)} %compare_select_fusion.order_ref, bf16[384,768]{1,0:T(8,128)(2,1)S(1)} %copy-done.9, bf16[384,768]{1,0:T(8,128)(2,1)S(1)} %copy-done.12, bf16[384,768]{1,0:T(8,128)(2,1)S(1)} %copy-done.14, ...), custom_call_target="tpu_custom_call", output_to_operand_aliasing={{0}: (8, {})} | custom-call | flops 7247757312 | bytes 21233664 | tf_op jit(solution)/shard_map/pallas_call | solution.py:212
  196.3 4.6 %collective-permute-start.25 = (bf16[384,1024]{1,0:T(8,128)(2,1)}, bf16[384,1024]{1,0:T(8,128)(2,1)S(1)}, u32[]{:S(2)}, u32[]{:S(2)}) collective-permute-start(bf16[384,1024]{1,0:T(8,128)(2,1)} %collective-permute-done.24.refs_2_), channel_id=1, source_target_pairs={{0,1},{1,2},{2,3},{3,0},{4,5},{5,6},{6,7},{7,4},{8,9},{9,10},{10,1... | collective-permute-start | bytes 2359304 | tf_op jit(solution)/shard_map/ppermute | solution.py:314
  204.3 8.8 %shard_map.153 = (bf16[3072,1536]{1,0:T(8,128)(2,1)S(1)}, f32[16,128]{1,0:T(8,128)S(1)}) custom-call(s32[4]{0:T(128)S(1)} %compare_select_fusion.order_ref, bf16[384,1024]{1,0:T(8,128)(2,1)S(1)} %get-tuple-element.80.refs_0_, bf16[384,1024]{1,0:T(8,128)(2,1)} %collective-permute-done.14.refs_1_, ...), custom_call_target="tpu_custom_call", output_to_operand_aliasing={{0}: (8, {})} | custom-call | flops 4831838208 | bytes 14155776 | tf_op jit(solution)/shard_map/pallas_call | solution.py:212
  213.0 4.3 %collective-permute-done.25.refs_3_ = bf16[384,1024]{1,0:T(8,128)(2,1)S(1)} collective-permute-done((bf16[384,1024]{1,0:T(8,128)(2,1)}, bf16[384,1024]{1,0:T(8,128)(2,1)S(1)}, u32[]{:S(2)}, u32[]{:S(2)}) %collective-permute-start.25) | collective-permute-done | bytes 786464 | tf_op jit(solution)/shard_map/ppermute | solution.py:314
  217.3 8.8 %shard_map.154 = (bf16[3072,1536]{1,0:T(8,128)(2,1)S(1)}, f32[16,128]{1,0:T(8,128)S(1)}) custom-call(s32[4]{0:T(128)S(1)} %compare_select_fusion.order_ref, bf16[384,1024]{1,0:T(8,128)(2,1)S(1)} %get-tuple-element.83.refs_0_, bf16[384,1024]{1,0:T(8,128)(2,1)} %collective-permute-done.16.refs_1_, ...), custom_call_target="tpu_custom_call", output_to_operand_aliasing={{0}: (8, {})} | custom-call | flops 4831838208 | bytes 14155776 | tf_op jit(solution)/shard_map/pallas_call | solution.py:212
  234.8 4.2 %collective-permute-start.32 = (f32[16,128]{1,0:T(8,128)S(1)}, f32[16,128]{1,0:T(8,128)S(1)}, u32[]{:S(2)}, u32[]{:S(2)}) collective-permute-start(f32[16,128]{1,0:T(8,128)S(1)} %add.59.refs_2_), channel_id=1, source_target_pairs={{0,3},{1,2},{2,1},{3,0},{4,7},{5,6},{6,5},{7,4},{8,11},{9,10},{10,... | collective-permute-start | bytes 24584 | tf_op jit(solution)/shard_map/ppermute | solution.py:27
  240.8 12.3 %shard_map.155 = (bf16[3072,1536]{1,0:T(8,128)(2,1)}, bf16[768,6144]{1,0:T(8,128)(2,1)}, f32[2]{0:T(128)}) custom-call(f32[2,2]{1,0:T(2,128)S(1)} %pad_maximum_fusion.factors_ref, f32[1,3840]{1,0:T(1,128)S(1)} %get-tuple-element.97.left_ref, f32[1,256]{1,0:T(1,128)S(1)} %slice.34.norms_ref, f32[1,1536]{1,0:T(1,128)S(1)} %get-tuple-element.105.refs_0_, ...), custom_call_target="tpu_custom_call" | custom-call | tf_op jit(solution)/shard_map/pallas_call | solution.py:277
  (147 shorter events, 77.1 us)
Async XLA Ops:
  7.2 130.7 %all-gather.5.cloned.1.call-start = ((), (), s32[]{:S(2)}) async-start(), calls=%async_computation.1 | async-start | bytes 5308416 | tf_op jit(solution)/shard_map/all_gather | solution.py:302
  7.9 150.1 %all-gather.3.cloned.1.call-start = ((), (), s32[]{:S(2)}) async-start(), calls=%async_computation | async-start | bytes 21233664 | tf_op jit(solution)/shard_map/all_gather | solution.py:302
  10.5 36.4 %collective-permute-start.1 = (bf16[384,1024]{1,0:T(8,128)(2,1)S(1)}, bf16[384,1024]{1,0:T(8,128)(2,1)S(1)}, u32[]{:S(2)}, u32[]{:S(2)}) collective-permute-start(bf16[384,1024]{1,0:T(8,128)(2,1)S(1)} %get-tuple-element.134.refs_0_), channel_id=1, source_target_pairs={{0,1},{1,2},{2,3},{3,0},{4,5},{5,6},{6,7},{7,4},{8,9},{9,10},{10,1... | collective-permute-start | bytes 2359304 | tf_op jit(solution)/shard_map/ppermute | solution.py:314
  13.6 33.3 %collective-permute-start = (bf16[384,768]{1,0:T(8,128)(2,1)}, bf16[384,768]{1,0:T(8,128)(2,1)S(1)}, u32[]{:S(2)}, u32[]{:S(2)}) collective-permute-start(bf16[384,768]{1,0:T(8,128)(2,1)} %refs_0_.3), channel_id=1, source_target_pairs={{0,1},{1,2},{2,3},{3,0},{4,5},{5,6},{6,7},{7,4},{8,9},{9,10},{10,1... | collective-permute-start | bytes 1769480 | tf_op jit(solution)/shard_map/ppermute | solution.py:314
  28.7 17.9 %collective-permute-start.2 = (f32[1,3840]{1,0:T(1,128)S(1)}, f32[1,3840]{1,0:T(1,128)S(1)}, u32[]{:S(2)}, u32[]{:S(2)}) collective-permute-start(f32[1,3840]{1,0:T(1,128)S(1)} %shard_map.144.refs_0_), channel_id=1, source_target_pairs={{0,1},{1,0},{2,3},{3,2},{4,5},{5,4},{6,7},{7,6},{8,9},{9,8},{10,11... | collective-permute-start | bytes 46088 | tf_op jit(solution)/shard_map/ppermute | solution.py:27
  30.4 16.5 %collective-permute-start.3 = (f32[1,3840]{1,0:T(1,128)S(1)}, f32[1,3840]{1,0:T(1,128)S(1)}, u32[]{:S(2)}, u32[]{:S(2)}) collective-permute-start(f32[1,3840]{1,0:T(1,128)S(1)} %shard_map.144.refs_0_), channel_id=1, source_target_pairs={{0,2},{1,3},{2,0},{3,1},{4,6},{5,7},{6,4},{7,5},{8,10},{9,11},{10,... | collective-permute-start | bytes 46088 | tf_op jit(solution)/shard_map/ppermute | solution.py:27
  31.8 15.1 %collective-permute-start.4 = (f32[1,3840]{1,0:T(1,128)S(1)}, f32[1,3840]{1,0:T(1,128)S(1)}, u32[]{:S(2)}, u32[]{:S(2)}) collective-permute-start(f32[1,3840]{1,0:T(1,128)S(1)} %shard_map.144.refs_0_), channel_id=1, source_target_pairs={{0,3},{1,2},{2,1},{3,0},{4,7},{5,6},{6,5},{7,4},{8,11},{9,10},{10,... | collective-permute-start | bytes 46088 | tf_op jit(solution)/shard_map/ppermute | solution.py:27
  46.9 18.1 %collective-permute-start.6 = (bf16[384,768]{1,0:T(8,128)(2,1)S(1)}, bf16[384,768]{1,0:T(8,128)(2,1)S(1)}, u32[]{:S(2)}, u32[]{:S(2)}) collective-permute-start(bf16[384,768]{1,0:T(8,128)(2,1)S(1)} %collective-permute-done.refs_1_), channel_id=1, source_target_pairs={{0,1},{1,2},{2,3},{3,0},{4,5},{5,6},{6,7},{7,4},{8,9},{9,10},{10,1... | collective-permute-start | bytes 1769480 | tf_op jit(solution)/shard_map/ppermute | solution.py:314
  47.8 46.5 %collective-permute-start.5 = (bf16[384,1024]{1,0:T(8,128)(2,1)S(1)}, bf16[384,1024]{1,0:T(8,128)(2,1)}, u32[]{:S(2)}, u32[]{:S(2)}) collective-permute-start(bf16[384,1024]{1,0:T(8,128)(2,1)S(1)} %collective-permute-done.1.refs_1_), channel_id=1, source_target_pairs={{0,1},{1,2},{2,3},{3,0},{4,5},{5,6},{6,7},{7,4},{8,9},{9,10},{10,1... | collective-permute-start | bytes 2359304 | tf_op jit(solution)/shard_map/ppermute | solution.py:314
  65.0 29.2 %collective-permute-start.10 = (bf16[384,768]{1,0:T(8,128)(2,1)S(1)}, bf16[384,768]{1,0:T(8,128)(2,1)S(1)}, u32[]{:S(2)}, u32[]{:S(2)}) collective-permute-start(bf16[384,768]{1,0:T(8,128)(2,1)S(1)} %collective-permute-done.6.refs_2_), channel_id=1, source_target_pairs={{0,1},{1,2},{2,3},{3,0},{4,5},{5,6},{6,7},{7,4},{8,9},{9,10},{10,1... | collective-permute-start | bytes 1769480 | tf_op jit(solution)/shard_map/ppermute | solution.py:314
  73.8 20.1 %collective-permute-start.11 = (f32[1,3840]{1,0:T(1,128)S(1)}, f32[1,3840]{1,0:T(1,128)S(1)}, u32[]{:S(2)}, u32[]{:S(2)}) collective-permute-start(f32[1,3840]{1,0:T(1,128)S(1)} %shard_map.147.refs_0_), channel_id=1, source_target_pairs={{0,1},{1,0},{2,3},{3,2},{4,5},{5,4},{6,7},{7,6},{8,9},{9,8},{10,11... | collective-permute-start | bytes 46088 | tf_op jit(solution)/shard_map/ppermute | solution.py:27
  75.3 19.0 %collective-permute-start.12 = (f32[1,3840]{1,0:T(1,128)S(1)}, f32[1,3840]{1,0:T(1,128)S(1)}, u32[]{:S(2)}, u32[]{:S(2)}) collective-permute-start(f32[1,3840]{1,0:T(1,128)S(1)} %shard_map.147.refs_0_), channel_id=1, source_target_pairs={{0,2},{1,3},{2,0},{3,1},{4,6},{5,7},{6,4},{7,5},{8,10},{9,11},{10,... | collective-permute-start | bytes 46088 | tf_op jit(solution)/shard_map/ppermute | solution.py:27
  78.2 16.0 %collective-permute-start.13 = (f32[1,3840]{1,0:T(1,128)S(1)}, f32[1,3840]{1,0:T(1,128)S(1)}, u32[]{:S(2)}, u32[]{:S(2)}) collective-permute-start(f32[1,3840]{1,0:T(1,128)S(1)} %shard_map.147.refs_0_), channel_id=1, source_target_pairs={{0,3},{1,2},{2,1},{3,0},{4,7},{5,6},{6,5},{7,4},{8,11},{9,10},{10,... | collective-permute-start | bytes 46088 | tf_op jit(solution)/shard_map/ppermute | solution.py:27
  95.1 22.6 %collective-permute-start.17 = (bf16[384,1024]{1,0:T(8,128)(2,1)}, bf16[384,1024]{1,0:T(8,128)(2,1)}, u32[]{:S(2)}, u32[]{:S(2)}) collective-permute-start(bf16[384,1024]{1,0:T(8,128)(2,1)} %collective-permute-done.5.refs_2_), channel_id=1, source_target_pairs={{0,1},{1,2},{2,3},{3,0},{4,5},{5,6},{6,7},{7,4},{8,9},{9,10},{10,1... | collective-permute-start | bytes 2359304 | tf_op jit(solution)/shard_map/ppermute | solution.py:314
  95.9 38.7 %collective-permute-start.14 = (bf16[384,1024]{1,0:T(8,128)(2,1)S(1)}, bf16[384,1024]{1,0:T(8,128)(2,1)}, u32[]{:S(2)}, u32[]{:S(2)}) collective-permute-start(bf16[384,1024]{1,0:T(8,128)(2,1)S(1)} %get-tuple-element.80.refs_0_), channel_id=1, source_target_pairs={{0,1},{1,2},{2,3},{3,0},{4,5},{5,6},{6,7},{7,4},{8,9},{9,10},{10,1... | collective-permute-start | bytes 2359304 | tf_op jit(solution)/shard_map/ppermute | solution.py:314
  108.1 47.2 %collective-permute-start.16 = (bf16[384,1024]{1,0:T(8,128)(2,1)S(1)}, bf16[384,1024]{1,0:T(8,128)(2,1)}, u32[]{:S(2)}, u32[]{:S(2)}) collective-permute-start(bf16[384,1024]{1,0:T(8,128)(2,1)S(1)} %get-tuple-element.83.refs_0_), channel_id=1, source_target_pairs={{0,1},{1,2},{2,3},{3,0},{4,5},{5,6},{6,7},{7,4},{8,9},{9,10},{10,1... | collective-permute-start | bytes 2359304 | tf_op jit(solution)/shard_map/ppermute | solution.py:314
  117.8 37.5 %collective-permute-start.21 = (f32[2,128]{1,0:T(2,128)S(1)}, f32[2,128]{1,0:T(2,128)S(1)}, u32[]{:S(2)}, u32[]{:S(2)}) collective-permute-start(f32[2,128]{1,0:T(2,128)S(1)} %get-tuple-element.99), channel_id=1, source_target_pairs={{0,1},{1,0},{2,3},{3,2},{4,5},{5,4},{6,7},{7,6},{8,9},{9,8},{10,11... | collective-permute-start | bytes 3080 | tf_op jit(solution)/shard_map/ppermute | solution.py:27
  117.9 37.4 %collective-permute-start.22 = (f32[2,128]{1,0:T(2,128)S(1)}, f32[2,128]{1,0:T(2,128)S(1)}, u32[]{:S(2)}, u32[]{:S(2)}) collective-permute-start(f32[2,128]{1,0:T(2,128)S(1)} %get-tuple-element.99), channel_id=1, source_target_pairs={{0,2},{1,3},{2,0},{3,1},{4,6},{5,7},{6,4},{7,5},{8,10},{9,11},{10,... | collective-permute-start | bytes 3080 | tf_op jit(solution)/shard_map/ppermute | solution.py:27
  118.0 37.3 %collective-permute-start.23 = (f32[2,128]{1,0:T(2,128)S(1)}, f32[2,128]{1,0:T(2,128)S(1)}, u32[]{:S(2)}, u32[]{:S(2)}) collective-permute-start(f32[2,128]{1,0:T(2,128)S(1)} %get-tuple-element.99), channel_id=1, source_target_pairs={{0,3},{1,2},{2,1},{3,0},{4,7},{5,6},{6,5},{7,4},{8,11},{9,10},{10,... | collective-permute-start | bytes 3080 | tf_op jit(solution)/shard_map/ppermute | solution.py:27
  134.7 42.3 %collective-permute-start.15 = (bf16[384,1024]{1,0:T(8,128)(2,1)}, bf16[384,1024]{1,0:T(8,128)(2,1)}, u32[]{:S(2)}, u32[]{:S(2)}) collective-permute-start(bf16[384,1024]{1,0:T(8,128)(2,1)} %collective-permute-done.14.refs_1_), channel_id=1, source_target_pairs={{0,1},{1,2},{2,3},{3,0},{4,5},{5,6},{6,7},{7,4},{8,9},{9,10},{10,1... | collective-permute-start | bytes 2359304 | tf_op jit(solution)/shard_map/ppermute | solution.py:314
  155.3 41.1 %collective-permute-start.24 = (bf16[384,1024]{1,0:T(8,128)(2,1)}, bf16[384,1024]{1,0:T(8,128)(2,1)}, u32[]{:S(2)}, u32[]{:S(2)}) collective-permute-start(bf16[384,1024]{1,0:T(8,128)(2,1)} %collective-permute-done.16.refs_1_), channel_id=1, source_target_pairs={{0,1},{1,2},{2,3},{3,0},{4,5},{5,6},{6,7},{7,4},{8,9},{9,10},{10,1... | collective-permute-start | bytes 2359304 | tf_op jit(solution)/shard_map/ppermute | solution.py:314
  177.0 24.9 %collective-permute-start.26 = (bf16[384,1024]{1,0:T(8,128)(2,1)}, bf16[384,1024]{1,0:T(8,128)(2,1)S(1)}, u32[]{:S(2)}, u32[]{:S(2)}) collective-permute-start(bf16[384,1024]{1,0:T(8,128)(2,1)} %collective-permute-done.15.refs_2_), channel_id=1, source_target_pairs={{0,1},{1,2},{2,3},{3,0},{4,5},{5,6},{6,7},{7,4},{8,9},{9,10},{10,1... | collective-permute-start | bytes 2359304 | tf_op jit(solution)/shard_map/ppermute | solution.py:314
  196.3 21.0 %collective-permute-start.25 = (bf16[384,1024]{1,0:T(8,128)(2,1)}, bf16[384,1024]{1,0:T(8,128)(2,1)S(1)}, u32[]{:S(2)}, u32[]{:S(2)}) collective-permute-start(bf16[384,1024]{1,0:T(8,128)(2,1)} %collective-permute-done.24.refs_2_), channel_id=1, source_target_pairs={{0,1},{1,2},{2,3},{3,0},{4,5},{5,6},{6,7},{7,4},{8,9},{9,10},{10,1... | collective-permute-start | bytes 2359304 | tf_op jit(solution)/shard_map/ppermute | solution.py:314
  234.8 5.9 %collective-permute-start.32 = (f32[16,128]{1,0:T(8,128)S(1)}, f32[16,128]{1,0:T(8,128)S(1)}, u32[]{:S(2)}, u32[]{:S(2)}) collective-permute-start(f32[16,128]{1,0:T(8,128)S(1)} %add.59.refs_2_), channel_id=1, source_target_pairs={{0,3},{1,2},{2,1},{3,0},{4,7},{5,6},{6,5},{7,4},{8,11},{9,10},{10,... | collective-permute-start | bytes 24584 | tf_op jit(solution)/shard_map/ppermute | solution.py:27
  (41 other events, 490.7 us)
Sparse Core Ops, SparseCore 0:
  9.9 41.6 all-gather.4
  53.4 99.4 all-gather.2

commit v3 on v2

--- a/solution.py
+++ b/solution.py
@@ -14,6 +14,18 @@
 BF16 = jnp.bfloat16
 
 
+def exchange(value, axis, size, stride=1):
+    return [value] + [
+        lax.ppermute(value, axis, [(i, i ^ k) for i in range(size)]) for k in range(stride, size, stride)
+    ]
+
+
+def tree(terms):
+    while len(terms) > 1:
+        terms = [terms[i] + terms[i + 1] for i in range(0, len(terms), 2)]
+    return terms[0]
+
+
 def all_sum(value, axis, size):
     step = 1
     while step < size:
@@ -22,16 +34,9 @@
     return value
 
 
-def exchange(value, axis, size):
-    return [value] + [
-        lax.ppermute(value, axis, [(i, i ^ k) for i in range(size)]) for k in range(1, size)
-    ]
-
-
-def tree(terms):
-    while len(terms) > 1:
-        terms = [terms[i] + terms[i + 1] for i in range(0, len(terms), 2)]
-    return terms[0]
+def quick_sum(value, axis, size):
+    pair = value + lax.ppermute(value, axis, [(i, i ^ 1) for i in range(size)])
+    return tree(exchange(pair, axis, size, 2))
 
 
 def fence(*values):
@@ -189,13 +194,12 @@
                     top += array.shape[1]
                     position += 1
 
-        here = slice(8 * which, 8 * which + 8)
         total = jnp.dot(turned[...], x_ref[...], preferred_element_type=F32)
         start = pl.multiple_of((first + pl.program_id(0)) * tile, LANES)
         g_ref[row : row + width, pl.ds(start, tile)] = total.astype(g_ref.dtype)
         product = total * w_ref[...].astype(F32)
         product = jnp.sum(product.reshape(-1, 8, tile), axis=0)
-        inner_ref[here, :] += sum(product[:, c : c + LANES] for c in range(0, tile, LANES))
+        inner_ref[8 * which : 8 * which + 8, :] += sum(product[:, c : c + LANES] for c in range(0, tile, LANES))
 
     in_specs = [pl.BlockSpec(array.shape, lambda j, o: (0, 0)) for array in flat]
     in_specs += [
@@ -203,7 +207,8 @@
         pl.BlockSpec((width, tile), lambda j, o: (chunk, first + j)),
         whole(inner),
     ]
-    operands = [order, *flat, inputs, weight, inner]
+    large = [pltpu.with_memory_space_constraint(array, pltpu.HBM) for array in (*flat, inputs, weight)]
+    operands = [order, *large, inner]
     aliases = {}
     if buffer is not None:
         in_specs.append(resident)
@@ -235,19 +240,16 @@
     )(*operands)
 
 
-def finish(grads, left, norms, rights, terms, factors):
+def finish(grads, lefts, rights, terms, factors):
     heights, steps = row_blocks(grads)
-    extents = [g.shape[0] for g in grads]
     spans = [g.shape[1] for g in grads]
     count = len(terms)
 
-    def kernel(factors_ref, left_ref, norms_ref, *refs):
-        right_refs, refs = refs[:2], refs[2:]
-        term_refs, refs = refs[:count], refs[count:]
-        g_refs, out_refs, gain_ref, v_refs = refs[:2], refs[2:4], refs[4], refs[5:]
-        step = pl.program_id(0)
-
-        @pl.when(step == 0)
+    def kernel(factors_ref, *refs):
+        right_refs, term_refs, refs = refs[:2], refs[2 : count + 2], refs[count + 2 :]
+        left_refs, g_refs, out_refs, gain_ref, v_refs = refs[:2], refs[2:4], refs[4:6], refs[6], refs[7:]
+
+        @pl.when(pl.program_id(0) == 0)
         def _():
             total = tree([ref[...] for ref in term_refs])
             for k in range(2):
@@ -256,33 +258,30 @@
                 gain_ref[k] = gw / sigma
                 v_refs[k][...] = gain * gw / (sigma * sigma) * right_refs[k][...]
 
-        row = 0
         for k in range(2):
             scale = factors_ref[0, k] / factors_ref[1, k]
-            top = pl.multiple_of(step * heights[k], LANES)
-            start = pl.multiple_of(row + step * heights[k], LANES)
-            norm = norm_of(norms_ref[:, k * LANES : (k + 1) * LANES])
-            column = column_of((left_ref[:, pl.ds(start, heights[k])] / norm).astype(BF16).astype(F32))
             for r in range(0, heights[k], 64):
-                part = column[r : r + 64]
+                part = left_refs[k][r : r + 64]
                 for c in range(0, spans[k], LANES):
                     here = slice(c, c + LANES)
-                    g = g_refs[k][pl.ds(top + r, 64), here].astype(F32)
+                    g = g_refs[k][r : r + 64, here].astype(F32)
                     out_refs[k][r : r + 64, here] = (scale * g - part * v_refs[k][:, here]).astype(BF16)
-            row += extents[k]
-
-    operands = [left, norms, *rights, *terms]
+
+    operands = [*rights, *terms]
     blocks = [pl.BlockSpec((heights[k], spans[k]), lambda i: (i, 0)) for k in range(2)]
     smem = pl.BlockSpec(memory_space=pltpu.SMEM)
     return pl.pallas_call(
         kernel,
         grid=(steps,),
-        in_specs=[smem] + [whole(o) for o in operands] + [pl.BlockSpec(memory_space=pltpu.VMEM)] * 2,
+        in_specs=[smem]
+        + [whole(o) for o in operands]
+        + [pl.BlockSpec((heights[k], LANES), lambda i: (i, 0)) for k in range(2)]
+        + blocks,
         out_specs=blocks + [smem],
         out_shape=[jax.ShapeDtypeStruct(g.shape, BF16) for g in grads] + [jax.ShapeDtypeStruct((2,), F32)],
         scratch_shapes=[pltpu.VMEM((1, span), F32) for span in spans],
-        compiler_params=pltpu.CompilerParams(vmem_limit_bytes=36 * 1024 * 1024),
-    )(factors, *operands, *grads)
+        compiler_params=pltpu.CompilerParams(vmem_limit_bytes=24 * 1024 * 1024),
+    )(factors, *operands, *lefts, *[pltpu.with_memory_space_constraint(g, pltpu.VMEM) for g in grads])
 
 
 def local(
@@ -299,14 +298,15 @@
     vector_down,
 ):
     weights = (weight_up, weight_down)
-    inputs = [lax.all_gather(array, "row", axis=0, tiled=True) for array in (inputs_up, inputs_down)]
+    all_down = lax.all_gather(inputs_down, "row", axis=0, tiled=True)
+    inputs = [lax.all_gather(inputs_up, "row", axis=0, tiled=True), all_down]
     extents = (weight_up.shape[0], weight_down.shape[0])
     spans = (weight_up.shape[1], weight_down.shape[1])
     ring = [(i, (i + 1) % cols) for i in range(cols)]
     order = lax.rem(lax.axis_index("col") - jnp.arange(cols, dtype=jnp.int32) + cols, jnp.int32(cols))
 
     third = grads_up.shape[1] // 3
-    held = {name: [grads_up[:, c * third : (c + 1) * third]] for c, name in enumerate("uvc")}
+    held = {"u": [grads_up[:, :third]]}
     held["d"] = [grads_down]
 
     def send(*names):
@@ -330,6 +330,8 @@
     send("d", "u")
     part = left_product((vector_up[None, :], vector_down[None, :]), weights)
     terms = exchange(part, "col", cols)
+    later, _ = fence(grads_up, part)
+    held["v"], held["c"] = [later[:, third : 2 * third]], [later[:, 2 * third :]]
     terms = when("du", terms)
     send("d", "u")
     left, total = right_product(terms, weights)
@@ -350,28 +352,29 @@
         send("u", "d", "v", "c")
     inner = when("v", inner)
     send("v")
-    inner = multiply(0, "u", 0, inner)
+    inner = multiply(1, "d", 0, inner, 0, 2)
     inner, squares = when("c", inner, squares)
     send("c")
     norms = total[:, sum(spans) :]
     norm = jnp.sqrt(jnp.sum(norms.reshape(2, LANES), axis=1) + EPS)
+    lefts = [left[0, : extents[0]] / norm[0], left[0, extents[0] :] / norm[1]]
+    columns = [jnp.broadcast_to(u.astype(BF16).astype(F32)[:, None], (u.shape[0], LANES)) for u in lefts]
     sigma = jnp.sqrt(jnp.sum(tree(squares), axis=1) + EPS)
-    vectors = [left[0, : extents[0]] / norm[0], left[0, extents[0] :] / norm[1]]
     rights = [rights[k] / sigma[k] for k in range(2)]
-    vectors += [row[0] for row in rights]
-    inner = multiply(1, "d", 0, inner, 0, 2)
-    inner, vectors, rights, sigma = when("v", inner, vectors, rights, sigma)
+    vectors = lefts + [row[0] for row in rights]
+    factors = jnp.stack([gain_pair, sigma])
+    inner = multiply(1, "d", 0, inner, 1, 2)
+    inner, vectors, rights, factors, columns = when("v", inner, vectors, rights, factors, columns)
     send("v")
-    inner = multiply(1, "d", 0, inner, 1, 2)
+    inner = multiply(0, "u", 0, inner)
     inner = when("c", inner)
     send("c")
     inner = when("v", inner)
     inner = multiply(0, "v", third, inner)
     inner = when("c", inner)
     inner = multiply(0, "c", 2 * third, inner)
-    terms = exchange(all_sum(inner, "row", rows), "col", cols)
-    factors = jnp.stack([gain_pair, sigma])
-    wgrad_up, wgrad_down, gain_grads = finish(grads, left, norms, rights, terms, factors)
+    terms = exchange(quick_sum(inner, "row", rows), "col", cols)
+    wgrad_up, wgrad_down, gain_grads = finish(grads, columns, rights, terms, factors)
     left_up, left_down, right_up, right_down = vectors
     return wgrad_up, wgrad_down, gain_grads, left_up, right_up, left_down, right_down
 

time: 261 us -> 257 us (0.985)
  local copies, waits for them, and re-layouts: 42 us -> 23 us
  waiting for transfers between devices: 76.4 us -> 93.3 us
    unnamed x60 -> x58, local copies, waits for them, and re-layouts: 38.3 us -> 18 us
    ppermute x12, waiting for transfers between devices: 26.3 us -> 45.4 us  [send(): held[name].append(lax.ppermute(held[name][-1], 'col', ring))]
    ppermute x9 -> x6, waiting for transfers between devices: 17.3 us -> 12.4 us  [all_sum(): lax.ppermute(value, axis, [(i, i ^ step) for i in range(size)])]
    pallas_call x5, Pallas kernels: 50.1 us -> 55 us  [grad_chunk(): pl.pallas_call(kernel, grid_spec=pltpu.PrefetchScalarGridSpec(num_scalar_...]
    ppermute x12 -> x15, starting transfers between devices: 17.7 us -> 21.6 us  [exchange(): lax.ppermute(value, axis, [(i, i ^ k) for i in range(size)])]
    ppermute x9 -> x6, starting transfers between devices: 9.44 us -> 6.4 us  [all_sum(): lax.ppermute(value, axis, [(i, i ^ step) for i in range(size)])]
    ppermute x12, starting transfers between devices: 13.4 us -> 10.5 us  [send(): held[name].append(lax.ppermute(held[name][-1], 'col', ring))]
    pallas_call x1, Pallas kernels: 12.3 us -> 9.49 us  [finish(): pl.pallas_call(kernel, grid=(steps,), in_specs=[smem] + [whole(o) for o i...]
  transfers between devices with their start and end apart: 35 -> 36, of which waited for: 20 -> 23; matrix products, arithmetic and copies ran while one was open for 3% -> 3% of each run, Pallas kernels for 23% -> 25%
where the time goes in v3:
time: 257 us
  waiting for transfers between devices  93.3 us (36%)
  Pallas kernels  83.6 us (33%)
  starting transfers between devices  38.6 us (15%)
  local copies, waits for them, and re-layouts  23 us (9%)
  between operations  14.5 us (6%)
  other arithmetic  3.74 us (1%)
    pallas_call x5, Pallas kernels, grad_chunk(): pl.pallas_call(kernel, grid_spec=pltpu.PrefetchScalarGridSpec(num_scalar_...  55 us
    ppermute x12, waiting for transfers between devices, send(): held[name].append(lax.ppermute(held[name][-1], 'col', ring))  45.4 us
    ppermute x15, waiting for transfers between devices, exchange(): lax.ppermute(value, axis, [(i, i ^ k) for i in range(size)])  33 us
    ppermute x15, starting transfers between devices, exchange(): lax.ppermute(value, axis, [(i, i ^ k) for i in range(size)])  21.6 us
    unnamed x58, local copies, waits for them, and re-layouts  18 us
    ppermute x6, waiting for transfers between devices, all_sum(): lax.ppermute(value, axis, [(i, i ^ step) for i in range(size)])  12.4 us
    ppermute x12, starting transfers between devices, send(): held[name].append(lax.ppermute(held[name][-1], 'col', ring))  10.5 us
    pallas_call x2, Pallas kernels, right_product(): pl.pallas_call(kernel, grid=(steps,), in_specs=[whole(t) for t in terms]...  9.52 us
  transfers between devices with their start and end apart: 36, of which 23 were waited for; matrix products, arithmetic and copies ran while one was open for 3% of the time, Pallas kernels for 25%

profile of v3, /device:TPU:0, one launch (start us, length us, event | category | flops | bytes accessed | tf_op | source)
XLA Modules:
  0.0 256.7 jit_solution(4047632524111896311)
XLA Ops:
  9.8 3.1 %collective-permute-start.1 = (bf16[384,1024]{1,0:T(8,128)(2,1)S(1)}, bf16[384,1024]{1,0:T(8,128)(2,1)S(1)}, u32[]{:S(2)}, u32[]{:S(2)}) collective-permute-start(bf16[384,1024]{1,0:T(8,128)(2,1)S(1)} %slice.30.refs_0_), channel_id=1, source_target_pairs={{0,1},{1,2},{2,3},{3,0},{4,5},{5,6},{6,7},{7,4},{8,9},{9,10},{10,1... | collective-permute-start | bytes 2359304 | tf_op jit(solution)/shard_map/ppermute | solution.py:314
  15.2 3.7 %copy-done = bf16[768,6144]{1,0:T(8,128)(2,1)S(1)} copy-done((bf16[768,6144]{1,0:T(8,128)(2,1)S(1)}, bf16[768,6144]{1,0:T(8,128)(2,1)}, u32[]{:S(2)}) %copy-start) | copy-done | bytes 9437208
  18.9 5.1 %copy-done.1 = bf16[3072,1536]{1,0:T(8,128)(2,1)S(1)} copy-done((bf16[3072,1536]{1,0:T(8,128)(2,1)S(1)}, bf16[3072,1536]{1,0:T(8,128)(2,1)}, u32[]{:S(2)}) %copy-start.1) | copy-done | bytes 9437208
  24.7 4.4 %shard_map.144.refs_0_ = f32[1,3840]{1,0:T(1,128)S(1)} custom-call(f32[1,1536]{1,0:T(1,128)S(1)} %broadcast_in_dim.10.v_up_ref, f32[1,6144]{1,0:T(1,128)S(1)} %bitcast.16, bf16[3072,1536]{1,0:T(8,128)(2,1)S(1)} %copy-done.1, bf16[768,6144]{1,0:T(8,128)(2,1)S(1)} %copy-done), custom_call_target="tpu_custom_call" | custom-call | tf_op jit(solution)/shard_map/pallas_call | solution.py:94
  33.5 12.4 %collective-permute-done.2.refs_1_ = f32[1,3840]{1,0:T(1,128)S(1)} collective-permute-done((f32[1,3840]{1,0:T(1,128)S(1)}, f32[1,3840]{1,0:T(1,128)S(1)}, u32[]{:S(2)}, u32[]{:S(2)}) %collective-permute-start.2) | collective-permute-done | bytes 15392 | tf_op jit(solution)/shard_map/ppermute | solution.py:19
  47.8 5.0 %shard_map.145 = (f32[1,3840]{1,0:T(1,128)}, f32[1,7936]{1,0:T(1,128)S(1)}) custom-call(f32[1,3840]{1,0:T(1,128)S(1)} %shard_map.144.refs_0_, f32[1,3840]{1,0:T(1,128)S(1)} %collective-permute-done.2.refs_1_, f32[1,3840]{1,0:T(1,128)S(1)} %collective-permute-done.3.refs_2_, f32[1,3840]{1,0:T(1,128)S(1)} %collective-permute-done.4.refs_3_, ...), custom_call_target="tpu_custom_call" | custom-call | tf_op jit(solution)/shard_map/pallas_call | solution.py:139
  65.1 3.8 %copy-done.2 = bf16[3072,1536]{1,0:T(8,128)(2,1)S(1)} copy-done((bf16[3072,1536]{1,0:T(8,128)(2,1)S(1)}, bf16[3072,1536]{1,0:T(8,128)(2,1)}, u32[]{:S(2)}) %copy-start.2) | copy-done | bytes 9437208
  68.9 4.3 %shard_map.147.refs_0_ = f32[1,3840]{1,0:T(1,128)S(1)} custom-call(f32[1,1536]{1,0:T(1,128)S(1)} %get-tuple-element.82.v_up_ref, f32[1,6144]{1,0:T(1,128)S(1)} %get-tuple-element.83.v_down_ref, bf16[3072,1536]{1,0:T(8,128)(2,1)S(1)} %copy-done.2, bf16[768,6144]{1,0:T(8,128)(2,1)S(1)} %bitcast.12), custom_call_target="tpu_custom_call" | custom-call | tf_op jit(solution)/shard_map/pallas_call | solution.py:94
  78.2 15.0 %collective-permute-done.11.refs_1_ = f32[1,3840]{1,0:T(1,128)S(1)} collective-permute-done((f32[1,3840]{1,0:T(1,128)S(1)}, f32[1,3840]{1,0:T(1,128)S(1)}, u32[]{:S(2)}, u32[]{:S(2)}) %collective-permute-start.11) | collective-permute-done | bytes 15392 | tf_op jit(solution)/shard_map/ppermute | solution.py:19
  94.5 4.5 %shard_map.149 = (f32[1,3840]{1,0:T(1,128)S(1)}, f32[1,7936]{1,0:T(1,128)S(1)}) custom-call(f32[1,3840]{1,0:T(1,128)S(1)} %shard_map.147.refs_0_, f32[1,3840]{1,0:T(1,128)S(1)} %collective-permute-done.11.refs_1_, f32[1,3840]{1,0:T(1,128)S(1)} %collective-permute-done.12.refs_2_, f32[1,3840]{1,0:T(1,128)S(1)} %collective-permute-done.13.refs_3_, ...), custom_call_target="tpu_custom_call" | custom-call | tf_op jit(solution)/shard_map/pallas_call | solution.py:139
  101.9 3.1 %collective-permute-done.19 = f32[1,7936]{1,0:T(1,128)S(1)} collective-permute-done((f32[1,7936]{1,0:T(1,128)S(1)}, f32[1,7936]{1,0:T(1,128)S(1)}, u32[]{:S(2)}, u32[]{:S(2)}) %collective-permute-start.19) | collective-permute-done | bytes 31776 | tf_op jit(solution)/shard_map/ppermute | solution.py:32
  109.7 6.3 %collective-permute-done.17.refs_3_ = bf16[384,1024]{1,0:T(8,128)(2,1)} collective-permute-done((bf16[384,1024]{1,0:T(8,128)(2,1)S(1)}, bf16[384,1024]{1,0:T(8,128)(2,1)}, u32[]{:S(2)}, u32[]{:S(2)}) %collective-permute-start.17) | collective-permute-done | bytes 786464 | tf_op jit(solution)/shard_map/ppermute | solution.py:314
  116.3 4.3 %collective-permute-start.23 = (f32[2,128]{1,0:T(2,128)S(1)}, f32[2,128]{1,0:T(2,128)S(1)}, u32[]{:S(2)}, u32[]{:S(2)}) collective-permute-start(f32[2,128]{1,0:T(2,128)S(1)} %get-tuple-element.103), channel_id=1, source_target_pairs={{0,3},{1,2},{2,1},{3,0},{4,7},{5,6},{6,5},{7,4},{8,11},{9,10},{10,... | collective-permute-start | bytes 3080 | tf_op jit(solution)/shard_map/ppermute | solution.py:19
  120.6 12.3 %collective-permute-done.14.refs_1_ = bf16[384,1024]{1,0:T(8,128)(2,1)} collective-permute-done((bf16[384,1024]{1,0:T(8,128)(2,1)S(1)}, bf16[384,1024]{1,0:T(8,128)(2,1)}, u32[]{:S(2)}, u32[]{:S(2)}) %collective-permute-start.14) | collective-permute-done | bytes 786464 | tf_op jit(solution)/shard_map/ppermute | solution.py:314
  135.1 13.3 %shard_map.148 = (bf16[768,6144]{1,0:T(8,128)(2,1)S(1)}, f32[16,128]{1,0:T(8,128)S(1)}) custom-call(s32[4]{0:T(128)S(1)} %compare_select_fusion.order_ref, bf16[384,768]{1,0:T(8,128)(2,1)} %refs_0_.3, bf16[384,768]{1,0:T(8,128)(2,1)} %copy-done.10, bf16[384,768]{1,0:T(8,128)(2,1)} %copy-done.11, bf16[384,768]{1,0:T(8,128)(2,1)} %copy-done.12, ...), custom_call_target="tpu_custom_call" | custom-call | flops 7247757312 | bytes 21233664 | tf_op jit(solution)/shard_map/pallas_call | solution.py:217
  151.7 12.5 %shard_map.151 = (bf16[768,6144]{1,0:T(8,128)(2,1)S(1)}, f32[16,128]{1,0:T(8,128)S(1)}) custom-call(s32[4]{0:T(128)S(1)} %compare_select_fusion.order_ref, bf16[384,768]{1,0:T(8,128)(2,1)} %refs_0_.3, bf16[384,768]{1,0:T(8,128)(2,1)} %copy-done.10, bf16[384,768]{1,0:T(8,128)(2,1)} %copy-done.11, ...), custom_call_target="tpu_custom_call", output_to_operand_aliasing={{0}: (8, {})} | custom-call | flops 7247757312 | bytes 21233664 | tf_op jit(solution)/shard_map/pallas_call | solution.py:217
  164.3 3.7 %copy-done.3 = bf16[768,6144]{1,0:T(8,128)(2,1)} copy-done((bf16[768,6144]{1,0:T(8,128)(2,1)}, bf16[768,6144]{1,0:T(8,128)(2,1)S(1)}, u32[]{:S(2)}) %copy-start.3) | copy-done | bytes 9437208
  171.7 9.5 %shard_map.152 = (bf16[3072,1536]{1,0:T(8,128)(2,1)S(1)}, f32[16,128]{1,0:T(8,128)S(1)}) custom-call(s32[4]{0:T(128)S(1)} %compare_select_fusion.order_ref, bf16[384,1024]{1,0:T(8,128)(2,1)} %copy-done.17, bf16[384,1024]{1,0:T(8,128)(2,1)} %copy-done.21, bf16[384,1024]{1,0:T(8,128)(2,1)} %copy-done.22, bf16[384,1024]{1,0:T(8,128)(2,1)} %collective-permute-done.17.refs_3_, ...), custom_call_target="tpu_custom_call" | custom-call | flops 4831838208 | bytes 14155776 | tf_op jit(solution)/shard_map/pallas_call | solution.py:217
  184.2 16.2 %collective-permute-done.26.refs_3_ = bf16[384,1024]{1,0:T(8,128)(2,1)} collective-permute-done((bf16[384,1024]{1,0:T(8,128)(2,1)S(1)}, bf16[384,1024]{1,0:T(8,128)(2,1)}, u32[]{:S(2)}, u32[]{:S(2)}) %collective-permute-start.26) | collective-permute-done | bytes 786464 | tf_op jit(solution)/shard_map/ppermute | solution.py:314
  200.4 9.8 %shard_map.153 = (bf16[3072,1536]{1,0:T(8,128)(2,1)S(1)}, f32[16,128]{1,0:T(8,128)S(1)}) custom-call(s32[4]{0:T(128)S(1)} %compare_select_fusion.order_ref, bf16[384,1024]{1,0:T(8,128)(2,1)} %copy-done.8, bf16[384,1024]{1,0:T(8,128)(2,1)} %collective-permute-done.14.refs_1_, bf16[384,1024]{1,0:T(8,128)(2,1)} %copy-done.14, ...), custom_call_target="tpu_custom_call", output_to_operand_aliasing={{0}: (8, {})} | custom-call | flops 4831838208 | bytes 14155776 | tf_op jit(solution)/shard_map/pallas_call | solution.py:217
  210.2 5.5 %collective-permute-done.25.refs_3_ = bf16[384,1024]{1,0:T(8,128)(2,1)S(1)} collective-permute-done((bf16[384,1024]{1,0:T(8,128)(2,1)S(1)}, bf16[384,1024]{1,0:T(8,128)(2,1)S(1)}, u32[]{:S(2)}, u32[]{:S(2)}) %collective-permute-start.25) | collective-permute-done | bytes 786464 | tf_op jit(solution)/shard_map/ppermute | solution.py:314
  216.6 9.8 %shard_map.154 = (bf16[3072,1536]{1,0:T(8,128)(2,1)S(1)}, f32[16,128]{1,0:T(8,128)S(1)}) custom-call(s32[4]{0:T(128)S(1)} %compare_select_fusion.order_ref, bf16[384,1024]{1,0:T(8,128)(2,1)} %copy-done.7, bf16[384,1024]{1,0:T(8,128)(2,1)} %copy-done.13, bf16[384,1024]{1,0:T(8,128)(2,1)} %copy-done.15, ...), custom_call_target="tpu_custom_call", output_to_operand_aliasing={{0}: (8, {})} | custom-call | flops 4831838208 | bytes 14155776 | tf_op jit(solution)/shard_map/pallas_call | solution.py:217
  234.3 4.3 %collective-permute-start.33 = (f32[16,128]{1,0:T(8,128)S(1)}, f32[16,128]{1,0:T(8,128)S(1)}, u32[]{:S(2)}, u32[]{:S(2)}) collective-permute-start(f32[16,128]{1,0:T(8,128)S(1)} %add_add_fusion.refs_2_), channel_id=1, source_target_pairs={{0,3},{1,2},{2,1},{3,0},{4,7},{5,6},{6,5},{7,4},{8,11},{9,10},{10,... | collective-permute-start | bytes 24584 | tf_op jit(solution)/shard_map/ppermute | solution.py:19
  240.4 9.5 %shard_map.155 = (bf16[3072,1536]{1,0:T(8,128)(2,1)}, bf16[768,6144]{1,0:T(8,128)(2,1)}, f32[2]{0:T(128)}) custom-call(f32[2,2]{1,0:T(2,128)S(1)} %pad_maximum_fusion.factors_ref, f32[1,1536]{1,0:T(1,128)S(1)} %get-tuple-element.109.refs_0_, f32[1,6144]{1,0:T(1,128)S(1)} %broadcast_divide_fusion.refs_1_, f32[16,128]{1,0:T(8,128)S(1)} %add_add_fusion.refs_2_, ...), custom_call_target="tpu_custom_call" | custom-call | tf_op jit(solution)/shard_map/pallas_call | solution.py:273
  (151 shorter events, 60.8 us)
Async XLA Ops:
  7.2 127.9 %all-gather.3.cloned.1.call-start = ((), (), s32[]{:S(2)}) async-start(), calls=%async_computation | async-start | bytes 21233664 | tf_op jit(solution)/shard_map/all_gather | solution.py:301
  7.9 163.8 %all-gather.5.cloned.1.call-start = ((), (), s32[]{:S(2)}) async-start(), calls=%async_computation.1 | async-start | bytes 5308416 | tf_op jit(solution)/shard_map/all_gather | solution.py:302
  9.8 36.4 %collective-permute-start.1 = (bf16[384,1024]{1,0:T(8,128)(2,1)S(1)}, bf16[384,1024]{1,0:T(8,128)(2,1)S(1)}, u32[]{:S(2)}, u32[]{:S(2)}) collective-permute-start(bf16[384,1024]{1,0:T(8,128)(2,1)S(1)} %slice.30.refs_0_), channel_id=1, source_target_pairs={{0,1},{1,2},{2,3},{3,0},{4,5},{5,6},{6,7},{7,4},{8,9},{9,10},{10,1... | collective-permute-start | bytes 2359304 | tf_op jit(solution)/shard_map/ppermute | solution.py:314
  12.9 33.3 %collective-permute-start = (bf16[384,768]{1,0:T(8,128)(2,1)}, bf16[384,768]{1,0:T(8,128)(2,1)S(1)}, u32[]{:S(2)}, u32[]{:S(2)}) collective-permute-start(bf16[384,768]{1,0:T(8,128)(2,1)} %refs_0_.3), channel_id=1, source_target_pairs={{0,1},{1,2},{2,3},{3,0},{4,5},{5,6},{6,7},{7,4},{8,9},{9,10},{10,1... | collective-permute-start | bytes 1769480 | tf_op jit(solution)/shard_map/ppermute | solution.py:314
  29.1 16.9 %collective-permute-start.2 = (f32[1,3840]{1,0:T(1,128)S(1)}, f32[1,3840]{1,0:T(1,128)S(1)}, u32[]{:S(2)}, u32[]{:S(2)}) collective-permute-start(f32[1,3840]{1,0:T(1,128)S(1)} %shard_map.144.refs_0_), channel_id=1, source_target_pairs={{0,1},{1,0},{2,3},{3,2},{4,5},{5,4},{6,7},{7,6},{8,9},{9,8},{10,11... | collective-permute-start | bytes 46088 | tf_op jit(solution)/shard_map/ppermute | solution.py:19
  30.8 15.5 %collective-permute-start.3 = (f32[1,3840]{1,0:T(1,128)S(1)}, f32[1,3840]{1,0:T(1,128)S(1)}, u32[]{:S(2)}, u32[]{:S(2)}) collective-permute-start(f32[1,3840]{1,0:T(1,128)S(1)} %shard_map.144.refs_0_), channel_id=1, source_target_pairs={{0,2},{1,3},{2,0},{3,1},{4,6},{5,7},{6,4},{7,5},{8,10},{9,11},{10,... | collective-permute-start | bytes 46088 | tf_op jit(solution)/shard_map/ppermute | solution.py:19
  31.9 14.4 %collective-permute-start.4 = (f32[1,3840]{1,0:T(1,128)S(1)}, f32[1,3840]{1,0:T(1,128)S(1)}, u32[]{:S(2)}, u32[]{:S(2)}) collective-permute-start(f32[1,3840]{1,0:T(1,128)S(1)} %shard_map.144.refs_0_), channel_id=1, source_target_pairs={{0,3},{1,2},{2,1},{3,0},{4,7},{5,6},{6,5},{7,4},{8,11},{9,10},{10,... | collective-permute-start | bytes 46088 | tf_op jit(solution)/shard_map/ppermute | solution.py:19
  46.3 18.1 %collective-permute-start.6 = (bf16[384,768]{1,0:T(8,128)(2,1)S(1)}, bf16[384,768]{1,0:T(8,128)(2,1)S(1)}, u32[]{:S(2)}, u32[]{:S(2)}) collective-permute-start(bf16[384,768]{1,0:T(8,128)(2,1)S(1)} %collective-permute-done.refs_1_), channel_id=1, source_target_pairs={{0,1},{1,2},{2,3},{3,0},{4,5},{5,6},{6,7},{7,4},{8,9},{9,10},{10,1... | collective-permute-start | bytes 1769480 | tf_op jit(solution)/shard_map/ppermute | solution.py:314
  47.1 46.5 %collective-permute-start.5 = (bf16[384,1024]{1,0:T(8,128)(2,1)S(1)}, bf16[384,1024]{1,0:T(8,128)(2,1)S(1)}, u32[]{:S(2)}, u32[]{:S(2)}) collective-permute-start(bf16[384,1024]{1,0:T(8,128)(2,1)S(1)} %collective-permute-done.1.refs_1_), channel_id=1, source_target_pairs={{0,1},{1,2},{2,3},{3,0},{4,5},{5,6},{6,7},{7,4},{8,9},{9,10},{10,1... | collective-permute-start | bytes 2359304 | tf_op jit(solution)/shard_map/ppermute | solution.py:314
  64.4 29.2 %collective-permute-start.10 = (bf16[384,768]{1,0:T(8,128)(2,1)S(1)}, bf16[384,768]{1,0:T(8,128)(2,1)S(1)}, u32[]{:S(2)}, u32[]{:S(2)}) collective-permute-start(bf16[384,768]{1,0:T(8,128)(2,1)S(1)} %collective-permute-done.6.refs_2_), channel_id=1, source_target_pairs={{0,1},{1,2},{2,3},{3,0},{4,5},{5,6},{6,7},{7,4},{8,9},{9,10},{10,1... | collective-permute-start | bytes 1769480 | tf_op jit(solution)/shard_map/ppermute | solution.py:314
  73.3 20.0 %collective-permute-start.11 = (f32[1,3840]{1,0:T(1,128)S(1)}, f32[1,3840]{1,0:T(1,128)S(1)}, u32[]{:S(2)}, u32[]{:S(2)}) collective-permute-start(f32[1,3840]{1,0:T(1,128)S(1)} %shard_map.147.refs_0_), channel_id=1, source_target_pairs={{0,1},{1,0},{2,3},{3,2},{4,5},{5,4},{6,7},{7,6},{8,9},{9,8},{10,11... | collective-permute-start | bytes 46088 | tf_op jit(solution)/shard_map/ppermute | solution.py:19
  75.7 17.9 %collective-permute-start.12 = (f32[1,3840]{1,0:T(1,128)S(1)}, f32[1,3840]{1,0:T(1,128)S(1)}, u32[]{:S(2)}, u32[]{:S(2)}) collective-permute-start(f32[1,3840]{1,0:T(1,128)S(1)} %shard_map.147.refs_0_), channel_id=1, source_target_pairs={{0,2},{1,3},{2,0},{3,1},{4,6},{5,7},{6,4},{7,5},{8,10},{9,11},{10,... | collective-permute-start | bytes 46088 | tf_op jit(solution)/shard_map/ppermute | solution.py:19
  77.7 15.9 %collective-permute-start.13 = (f32[1,3840]{1,0:T(1,128)S(1)}, f32[1,3840]{1,0:T(1,128)S(1)}, u32[]{:S(2)}, u32[]{:S(2)}) collective-permute-start(f32[1,3840]{1,0:T(1,128)S(1)} %shard_map.147.refs_0_), channel_id=1, source_target_pairs={{0,3},{1,2},{2,1},{3,0},{4,7},{5,6},{6,5},{7,4},{8,11},{9,10},{10,... | collective-permute-start | bytes 46088 | tf_op jit(solution)/shard_map/ppermute | solution.py:19
  93.6 22.4 %collective-permute-start.17 = (bf16[384,1024]{1,0:T(8,128)(2,1)S(1)}, bf16[384,1024]{1,0:T(8,128)(2,1)}, u32[]{:S(2)}, u32[]{:S(2)}) collective-permute-start(bf16[384,1024]{1,0:T(8,128)(2,1)S(1)} %collective-permute-done.5.refs_2_), channel_id=1, source_target_pairs={{0,1},{1,2},{2,3},{3,0},{4,5},{5,6},{6,7},{7,4},{8,9},{9,10},{10,1... | collective-permute-start | bytes 2359304 | tf_op jit(solution)/shard_map/ppermute | solution.py:314
  94.5 38.5 %collective-permute-start.14 = (bf16[384,1024]{1,0:T(8,128)(2,1)S(1)}, bf16[384,1024]{1,0:T(8,128)(2,1)}, u32[]{:S(2)}, u32[]{:S(2)}) collective-permute-start(bf16[384,1024]{1,0:T(8,128)(2,1)S(1)} %get-tuple-element.84.refs_0_), channel_id=1, source_target_pairs={{0,1},{1,2},{2,3},{3,0},{4,5},{5,6},{6,7},{7,4},{8,9},{9,10},{10,1... | collective-permute-start | bytes 2359304 | tf_op jit(solution)/shard_map/ppermute | solution.py:314
  106.7 43.0 %collective-permute-start.16 = (bf16[384,1024]{1,0:T(8,128)(2,1)S(1)}, bf16[384,1024]{1,0:T(8,128)(2,1)S(1)}, u32[]{:S(2)}, u32[]{:S(2)}) collective-permute-start(bf16[384,1024]{1,0:T(8,128)(2,1)S(1)} %get-tuple-element.87.refs_0_), channel_id=1, source_target_pairs={{0,1},{1,2},{2,3},{3,0},{4,5},{5,6},{6,7},{7,4},{8,9},{9,10},{10,1... | collective-permute-start | bytes 2359304 | tf_op jit(solution)/shard_map/ppermute | solution.py:314
  116.2 33.5 %collective-permute-start.21 = (f32[2,128]{1,0:T(2,128)S(1)}, f32[2,128]{1,0:T(2,128)S(1)}, u32[]{:S(2)}, u32[]{:S(2)}) collective-permute-start(f32[2,128]{1,0:T(2,128)S(1)} %get-tuple-element.103), channel_id=1, source_target_pairs={{0,1},{1,0},{2,3},{3,2},{4,5},{5,4},{6,7},{7,6},{8,9},{9,8},{10,11... | collective-permute-start | bytes 3080 | tf_op jit(solution)/shard_map/ppermute | solution.py:19
  116.3 33.4 %collective-permute-start.22 = (f32[2,128]{1,0:T(2,128)S(1)}, f32[2,128]{1,0:T(2,128)S(1)}, u32[]{:S(2)}, u32[]{:S(2)}) collective-permute-start(f32[2,128]{1,0:T(2,128)S(1)} %get-tuple-element.103), channel_id=1, source_target_pairs={{0,2},{1,3},{2,0},{3,1},{4,6},{5,7},{6,4},{7,5},{8,10},{9,11},{10,... | collective-permute-start | bytes 3080 | tf_op jit(solution)/shard_map/ppermute | solution.py:19
  116.3 33.4 %collective-permute-start.23 = (f32[2,128]{1,0:T(2,128)S(1)}, f32[2,128]{1,0:T(2,128)S(1)}, u32[]{:S(2)}, u32[]{:S(2)}) collective-permute-start(f32[2,128]{1,0:T(2,128)S(1)} %get-tuple-element.103), channel_id=1, source_target_pairs={{0,3},{1,2},{2,1},{3,0},{4,7},{5,6},{6,5},{7,4},{8,11},{9,10},{10,... | collective-permute-start | bytes 3080 | tf_op jit(solution)/shard_map/ppermute | solution.py:19
  132.9 36.3 %collective-permute-start.15 = (bf16[384,1024]{1,0:T(8,128)(2,1)}, bf16[384,1024]{1,0:T(8,128)(2,1)S(1)}, u32[]{:S(2)}, u32[]{:S(2)}) collective-permute-start(bf16[384,1024]{1,0:T(8,128)(2,1)} %collective-permute-done.14.refs_1_), channel_id=1, source_target_pairs={{0,1},{1,2},{2,3},{3,0},{4,5},{5,6},{6,7},{7,4},{8,9},{9,10},{10,1... | collective-permute-start | bytes 2359304 | tf_op jit(solution)/shard_map/ppermute | solution.py:314
  149.7 33.7 %collective-permute-start.24 = (bf16[384,1024]{1,0:T(8,128)(2,1)S(1)}, bf16[384,1024]{1,0:T(8,128)(2,1)S(1)}, u32[]{:S(2)}, u32[]{:S(2)}) collective-permute-start(bf16[384,1024]{1,0:T(8,128)(2,1)S(1)} %collective-permute-done.16.refs_1_), channel_id=1, source_target_pairs={{0,1},{1,2},{2,3},{3,0},{4,5},{5,6},{6,7},{7,4},{8,9},{9,10},{10,1... | collective-permute-start | bytes 2359304 | tf_op jit(solution)/shard_map/ppermute | solution.py:314
  171.0 29.3 %collective-permute-start.26 = (bf16[384,1024]{1,0:T(8,128)(2,1)S(1)}, bf16[384,1024]{1,0:T(8,128)(2,1)}, u32[]{:S(2)}, u32[]{:S(2)}) collective-permute-start(bf16[384,1024]{1,0:T(8,128)(2,1)S(1)} %collective-permute-done.15.refs_2_), channel_id=1, source_target_pairs={{0,1},{1,2},{2,3},{3,0},{4,5},{5,6},{6,7},{7,4},{8,9},{9,10},{10,1... | collective-permute-start | bytes 2359304 | tf_op jit(solution)/shard_map/ppermute | solution.py:314
  183.4 32.3 %collective-permute-start.25 = (bf16[384,1024]{1,0:T(8,128)(2,1)S(1)}, bf16[384,1024]{1,0:T(8,128)(2,1)S(1)}, u32[]{:S(2)}, u32[]{:S(2)}) collective-permute-start(bf16[384,1024]{1,0:T(8,128)(2,1)S(1)} %collective-permute-done.24.refs_2_), channel_id=1, source_target_pairs={{0,1},{1,2},{2,3},{3,0},{4,5},{5,6},{6,7},{7,4},{8,9},{9,10},{10,1... | collective-permute-start | bytes 2359304 | tf_op jit(solution)/shard_map/ppermute | solution.py:314
  234.3 6.0 %collective-permute-start.33 = (f32[16,128]{1,0:T(8,128)S(1)}, f32[16,128]{1,0:T(8,128)S(1)}, u32[]{:S(2)}, u32[]{:S(2)}) collective-permute-start(f32[16,128]{1,0:T(8,128)S(1)} %add_add_fusion.refs_2_), channel_id=1, source_target_pairs={{0,3},{1,2},{2,1},{3,0},{4,7},{5,6},{6,5},{7,4},{8,11},{9,10},{10,... | collective-permute-start | bytes 24584 | tf_op jit(solution)/shard_map/ppermute | solution.py:19
  (41 other events, 589.5 us)
Sparse Core Ops, SparseCore 0:
  9.9 102.7 all-gather.2
  114.6 38.9 all-gather.4
